TPU v7x, 256 devices: a whole 4x4x8 slice. The times are simulated.
256 devices in a mesh: gx: 32 (over z_hi, x, y), gy: 8 (over z_lo, core).
Axes of the slice: x: 4, y: 4, z: 8 (z_hi: 2, z_lo: 4; z = z_hi * 4 + z_lo), core: 2. Of those that a mesh axis runs over, the one named last changes fastest.
Arguments:
- bead_charge: float32 [32, 8, 16384], P('gx', 'gy'), may hold values from -6 to 6
- bead_cell: int32 [32, 8, 16384], P('gx', 'gy'), may hold values from 0 to 32767
- bead_count: int32 [32, 8], P('gx', 'gy'), may hold values from 8192 to 16384
- interp_weights: bfloat16 [32, 8, 12, 16384], P('gx', 'gy'), may hold values from 0.049804688 to 0.59765625
- kernel_fine: bfloat16 [17, 17, 17], replicated, may hold values from 0 to 4
- kernel_coarse: bfloat16 [17, 17, 17], replicated, may hold values from 0 to 4
Outputs:
- bead_potential: float32 [32, 8, 16384], P('gx', 'gy')
- potential_grid: float32 [512, 128, 128], P('gx', 'gy')
All inputs are finite; a program needn't handle non-finite values.
Results may differ from a plain program's by a relative error of at most 0.00076.
Values may be sent and summed in bfloat16 or wider, within the bound.
A program may use at most 64 MiB of HBM per device.

v0:
```python
import functools

import jax
import jax.numpy as jnp
from jax import lax
from jax.experimental import pallas as pl
from jax.experimental.pallas import tpu as pltpu
from jax.sharding import PartitionSpec as P

LX = 16
LY = 16
LZ = 128
SIDE = 17
BLOCK = 1024
ROWS = 384
MESH = pl.DeviceIdType.MESH
F32 = jnp.float32
BF16 = jnp.bfloat16
LANES_BOTH = (((1,), (1,)), ((), ()))


def iota(shape, dim):
    return lax.broadcasted_iota(jnp.int32, shape, dim)


def split(value):
    high = value.astype(BF16)
    low = (value - high.astype(F32)).astype(BF16)
    return high, low


def bead_tables(cells, weights, scale):
    count = cells.shape[1]
    first = cells >> 11
    second = (cells >> 7) & 15
    third = cells & 127
    rows = iota((24, count), 0)
    away_first = rows - first
    away_second = rows - second
    rows_first = jnp.zeros((24, count), F32)
    rows_second = jnp.zeros((24, count), F32)
    for tap in range(4):
        amount = weights[tap : tap + 1]
        if scale is not None:
            amount = amount * scale
        rows_first = jnp.where(away_first == tap, amount, rows_first)
        rows_second = jnp.where(away_second == tap, weights[4 + tap : 5 + tap], rows_second)
    depth = jnp.zeros((LZ, count), F32)
    away = (iota((LZ, count), 0) - third) & 127
    for tap in range(4):
        depth = jnp.where(away == tap, weights[8 + tap : 9 + tap], depth)
    return rows_first, rows_second, depth.astype(BF16)


def spread_kernel(count_ref, charge_ref, cell_ref, weight_ref, main_ref, tail_ref, total):
    live = count_ref[0, 0]
    total[...] = jnp.zeros_like(total)

    def add_block(step, carry):
        start = pl.multiple_of(step * BLOCK, BLOCK)
        here = pl.ds(start, BLOCK)
        slots = iota((1, BLOCK), 1) + start
        charge = jnp.where(slots < live, charge_ref[:, here], 0.0)
        weights = weight_ref[:, here].astype(F32)
        rows_first, rows_second, depth = bead_tables(cell_ref[:, here], weights, charge)
        parts = [rows_first[x : x + 1] * rows_second[:16] for x in range(19)]
        parts += [rows_second[y : y + 1] * rows_first for y in range(16, 19)]
        parts += [jnp.zeros((8, BLOCK), F32)]
        high, low = split(jnp.concatenate(parts, axis=0))
        total[...] += lax.dot_general(
            high, depth, LANES_BOTH, preferred_element_type=F32
        ) + lax.dot_general(low, depth, LANES_BOTH, preferred_element_type=F32)
        return carry

    lax.fori_loop(0, charge_ref.shape[1] // BLOCK, add_block, 0)
    main_ref[...] = total[0:304].reshape(19, 16, LZ)
    tail_ref[...] = total[304:376].reshape(3, 24, LZ)


def read_kernel(count_ref, cell_ref, weight_ref, main_ref, tail_ref, bead_ref, grid_ref, table):
    live = count_ref[0, 0]
    grid_ref[...] = main_ref[0:16]
    flat = jnp.concatenate(
        [main_ref[...].reshape(304, LZ), tail_ref[...].reshape(72, LZ), jnp.zeros((8, LZ), F32)],
        axis=0,
    )
    high, low = split(flat)
    table[:, 0:LZ] = high
    table[:, LZ:] = low

    def read_block(step, carry):
        start = pl.multiple_of(step * BLOCK, BLOCK)
        here = pl.ds(start, BLOCK)
        weights = weight_ref[:, here].astype(F32)
        rows_first, rows_second, depth = bead_tables(cell_ref[:, here], weights, None)
        along = jnp.dot(
            table[...], jnp.concatenate([depth, depth], axis=0), preferred_element_type=F32
        )
        near = jnp.zeros((16, BLOCK), F32)
        for x in range(19):
            near = near + rows_first[x : x + 1] * along[16 * x : 16 * x + 16]
        far = jnp.zeros((24, BLOCK), F32)
        for y in range(3):
            far = far + rows_second[16 + y : 17 + y] * along[304 + 24 * y : 328 + 24 * y]
        near = near * rows_second[:16]
        far = far * rows_first
        both = near[:8] + near[8:] + far[:8] + far[8:16] + far[16:]
        slots = iota((1, BLOCK), 1) + start
        value = jnp.sum(both, axis=0, keepdims=True)
        bead_ref[:, here] = jnp.where(slots < live, value, 0.0)
        return carry

    lax.fori_loop(0, cell_ref.shape[1] // BLOCK, read_block, 0)


AROUND = [(a, b) for a in (-1, 0, 1) for b in (-1, 0, 1) if (a, b) != (0, 0)]


def middle_kernel(
    sizes,
    main_ref,
    tail_ref,
    fine_ref,
    coarse_ref,
    pmain_ref,
    ptail_ref,
    side_first,
    side_second,
    side_both,
    charges,
    out_edge,
    out_corner,
    in_edge,
    in_corner,
    grid,
    shifted,
    summed,
    lines,
    fine_table,
    coarse_table,
    own_coarse,
    in_coarse,
    wide_coarse,
    shifted_coarse,
    total,
    own_pot,
    in_pot,
    wide_pot,
    rows_pot,
    send_tail,
    potential,
    send_1,
    recv_1,
    send_2,
    recv_2,
    send_3,
    recv_3,
    send_4,
    recv_4,
    send_5,
    recv_5,
):
    here_first = lax.axis_index("gx")
    here_second = lax.axis_index("gy")

    def device(a, b):
        return (
            lax.rem(here_first + (a + sizes[0]), sizes[0]),
            lax.rem(here_second + (b + sizes[1]), sizes[1]),
        )

    def send(source, target, out_sem, in_sem, a, b):
        copy = pltpu.make_async_remote_copy(
            src_ref=source,
            dst_ref=target,
            send_sem=out_sem,
            recv_sem=in_sem,
            device_id=device(a, b),
            device_id_type=MESH,
        )
        copy.start()
        return copy

    barrier = pltpu.get_barrier_semaphore()
    for a, b in AROUND:
        pl.semaphore_signal(barrier, inc=1, device_id=device(a, b), device_id_type=MESH)
    pl.semaphore_wait(barrier, 8)

    spills = [
        send(main_ref.at[16:19], side_first, send_1.at[0], recv_1.at[0], 1, 0),
        send(tail_ref.at[:, 0:16], side_second, send_1.at[1], recv_1.at[1], 0, 1),
        send(tail_ref.at[:, 16:24], side_both, send_1.at[2], recv_1.at[2], 1, 1),
    ]

    taps = iota((SIDE, LZ), 0)
    lanes = iota((SIDE, LZ), 1)
    place_fine = (((lanes + taps - 8) & 127) == 0).astype(BF16)
    place_coarse = (((lanes + taps - 8) & 63) == 0).astype(BF16)
    lines[18, 0:SIDE] = jnp.zeros((SIDE, LZ), F32)
    lines[36, 0:SIDE] = jnp.zeros((SIDE, LZ), F32)
    for dx in range(SIDE):
        lines[dx, 0:SIDE] = jnp.dot(fine_ref[dx], place_fine, preferred_element_type=F32)
        lines[19 + dx, 0:SIDE] = jnp.dot(coarse_ref[dx], place_coarse, preferred_element_type=F32)

    def first_rows(line):
        return pltpu.roll(
            jnp.broadcast_to(line, (8, LZ)), 0, 1, stride=1, stride_axis=0
        )

    def turned(base, shift):
        return base if shift == 0 else pltpu.roll(base, shift, 1)

    def build_fine(dx, carry):
        for dy in range(SIDE):
            base = first_rows(lines[dx, dy : dy + 1])
            rows = [turned(base, 8 * i) for i in range(16)]
            fine_table[dx, 128 * dy : 128 * dy + 128] = jnp.concatenate(rows, axis=0).astype(BF16)
        return carry

    lax.fori_loop(0, SIDE, build_fine, 0)

    for copy in spills:
        copy.wait()
    charges[...] = main_ref[0:16]
    charges[0:3] += side_first[...]
    for y in range(3):
        side_second[y, 0:8] += side_both[y]
        charges[:, y, :] += side_second[y]
    rounded = charges[...].astype(BF16).astype(F32)
    grid[8:24, 8:24] = rounded

    halves = [grid[8:24, 8:16], grid[8:24, 16:24]]
    out_edge[0] = grid[8:16, 8:24].astype(BF16)
    out_edge[1] = grid[16:24, 8:24].astype(BF16)
    out_edge[2] = halves[0].reshape(8, 16, LZ).astype(BF16)
    out_edge[3] = halves[1].reshape(8, 16, LZ).astype(BF16)
    for i in range(2):
        for j in range(2):
            quarter = grid[8 + 8 * i : 16 + 8 * i, 8 + 8 * j : 16 + 8 * j]
            out_corner[2 * i + j] = quarter.reshape(4, 16, LZ).astype(BF16)
    halos = []
    for at, (a, b) in enumerate([(-1, 0), (1, 0), (0, -1), (0, 1)]):
        halos.append(send(out_edge.at[at], in_edge.at[at], send_2.at[at], recv_2.at[at], a, b))
    for at, (a, b) in enumerate([(-1, -1), (-1, 1), (1, -1), (1, 1)]):
        halos.append(
            send(out_corner.at[at], in_corner.at[at], send_2.at[4 + at], recv_2.at[4 + at], a, b)
        )

    lower_half = iota((64, LZ), 1) < 64

    def build_coarse(m, carry):
        for dy in range(SIDE):
            blocks = []
            for step in range(3):
                base = first_rows(lines[18 + 2 * m + step, dy : dy + 1])
                blocks.append(jnp.concatenate([turned(base, 8 * i) for i in range(8)], axis=0))
            pair = [
                jnp.where(lower_half, blocks[1], blocks[0]),
                jnp.where(lower_half, blocks[2], blocks[1]),
            ]
            coarse_table[m, 128 * dy : 128 * dy + 128] = jnp.concatenate(pair, axis=0).astype(BF16)
        return carry

    lax.fori_loop(0, 9, build_coarse, 0)

    for copy in halos:
        copy.wait()
    grid[24:32, 8:24] = in_edge[0].astype(F32)
    grid[0:8, 8:24] = in_edge[1].astype(F32)
    grid[8:24, 24:32] = in_edge[2].astype(F32).reshape(16, 8, LZ)
    grid[8:24, 0:8] = in_edge[3].astype(F32).reshape(16, 8, LZ)
    for i in range(2):
        for j in range(2):
            quarter = in_corner[2 * i + j].astype(F32).reshape(8, 8, LZ)
            grid[24 - 24 * i : 32 - 24 * i, 24 - 24 * j : 32 - 24 * j] = quarter

    gap = (iota((LZ, LZ), 0) - 2 * (iota((LZ, LZ), 1) & 63) + 2) & 127
    spline = jnp.where(gap == 2, 0.75, 0.0)
    spline = jnp.where((gap == 1) | (gap == 3), 0.5, spline)
    spline = jnp.where((gap == 0) | (gap == 4), 0.125, spline).astype(BF16)
    coarse_lines = jnp.dot(
        grid[6:25].reshape(19 * 32, LZ).astype(BF16), spline, preferred_element_type=F32
    ).reshape(19, 32, LZ)
    for i in range(8):
        summed[i] = (
            0.125 * (coarse_lines[2 * i] + coarse_lines[2 * i + 4])
            + 0.5 * (coarse_lines[2 * i + 1] + coarse_lines[2 * i + 3])
            + 0.75 * coarse_lines[2 * i + 2]
        )
    lower_8 = iota((8, LZ), 1) < 64
    for j in range(4):
        planes = []
        for i in (2 * j, 2 * j + 1):
            parts = [summed[i, pl.ds(6 + t, 8, stride=2)] for t in range(5)]
            planes.append(
                0.125 * (parts[0] + parts[4]) + 0.5 * (parts[1] + parts[3]) + 0.75 * parts[2]
            )
        own_coarse[j] = jnp.where(lower_8, planes[0], planes[1]).astype(BF16).astype(F32)
    coarse_sends = []
    for at, (a, b) in enumerate(AROUND):
        coarse_sends.append(send(own_coarse, in_coarse.at[at], send_3.at[at], recv_3.at[at], a, b))

    for dy in range(SIDE):
        shifted[dy] = grid[:, dy : dy + 16].astype(BF16)
    total[...] = jnp.zeros_like(total)

    def correlate_fine(dx, carry):
        acc = total[...]
        for dy in range(0, SIDE, 2):
            depth = min(2, SIDE - dy)
            left = [shifted[dy + k, pl.ds(dx, 16)].reshape(256, LZ) for k in range(depth)]
            acc = acc + jnp.dot(
                jnp.concatenate(left, axis=1),
                fine_table[dx, 128 * dy : 128 * (dy + depth)],
                preferred_element_type=F32,
            )
        total[...] = acc
        return carry

    lax.fori_loop(0, 9, correlate_fine, 0)

    for copy in coarse_sends:
        copy.wait()
    wide_coarse[4:8, 8:16] = own_coarse[...]
    for at, (a, b) in enumerate(AROUND):
        wide_coarse[4 - 4 * a : 8 - 4 * a, 8 - 8 * b : 16 - 8 * b] = in_coarse[at]
    for dy in range(SIDE):
        shifted_coarse[dy] = wide_coarse[:, dy : dy + 8]

    def correlate_coarse(m, acc):
        for dy in range(0, SIDE, 2):
            depth = min(2, SIDE - dy)
            left = [
                shifted_coarse[dy + k, pl.ds(m, 4)].reshape(32, LZ).astype(BF16)
                for k in range(depth)
            ]
            acc = acc + jnp.dot(
                jnp.concatenate(left, axis=1),
                coarse_table[m, 128 * dy : 128 * (dy + depth)],
                preferred_element_type=F32,
            )
        return acc

    own_pot[...] = lax.fori_loop(0, 9, correlate_coarse, jnp.zeros((32, LZ), F32)).reshape(
        4, 8, LZ
    )
    pot_sends = []
    for at, (a, b) in enumerate(AROUND):
        span = slice(0, 4) if a == 0 else (slice(0, 1) if a < 0 else slice(3, 4))
        land = slice(0, 4) if a == 0 else slice(0, 1)
        pot_sends.append(
            send(own_pot.at[span], in_pot.at[at, land], send_4.at[at], recv_4.at[at], a, b)
        )

    lax.fori_loop(9, SIDE, correlate_fine, 0)

    for copy in pot_sends:
        copy.wait()
    wide_pot[1:5, 8:16] = own_pot[...]
    for at, (a, b) in enumerate(AROUND):
        first = slice(1, 5) if a == 0 else (slice(5, 6) if a < 0 else slice(0, 1))
        land = slice(0, 4) if a == 0 else slice(0, 1)
        wide_pot[first, 8 - 8 * b : 16 - 8 * b] = in_pot[at, land]
    planes = [pltpu.roll(wide_pot[0], 64, 1)]
    for j in range(1, 5):
        planes += [wide_pot[j], pltpu.roll(wide_pot[j], 64, 1)]
    planes += [wide_pot[5]]
    for i in range(8):
        rows_pot[2 * i] = (planes[i] + 6.0 * planes[i + 1] + planes[i + 2]) * 0.125
        rows_pot[2 * i + 1] = (planes[i + 1] + planes[i + 2]) * 0.5
    below = rows_pot[:, 7:15]
    middle = rows_pot[:, 8:16]
    above = rows_pot[:, 9:17]
    even_rows = (below + 6.0 * middle + above) * 0.125
    odd_rows = (middle + above) * 0.5
    for i in range(16):
        potential[i, pl.ds(0, 8, stride=2)] = even_rows[i]
        potential[i, pl.ds(1, 8, stride=2)] = odd_rows[i]
    source = iota((LZ, LZ), 0)
    offset = (iota((LZ, LZ), 1) - 2 * source + 1) & 127
    refine = jnp.where((offset == 0) | (offset == 2), 0.5, 0.0)
    refine = jnp.where(offset == 1, 0.75, refine)
    far = (iota((LZ, LZ), 1) - 2 * source + 2) & 127
    refine = jnp.where((far == 0) | (far == 4), 0.125, refine)
    refine = jnp.where(source < 64, refine, 0.0).astype(BF16)
    high, low = split(potential[...].reshape(256, LZ))
    smooth = jnp.dot(
        jnp.concatenate([high, low], axis=1),
        jnp.concatenate([refine, refine], axis=0),
        preferred_element_type=F32,
    )
    potential[...] = (total[...] + smooth).reshape(16, 16, LZ)

    for y in range(3):
        send_tail[y] = potential[:, y, :]
    upper = [
        send(potential.at[0:3], pmain_ref.at[16:19], send_5.at[0], recv_5.at[0], -1, 0),
        send(send_tail, ptail_ref.at[:, 0:16], send_5.at[1], recv_5.at[1], 0, -1),
        send(send_tail.at[:, 0:8], ptail_ref.at[:, 16:24], send_5.at[2], recv_5.at[2], -1, -1),
    ]
    pmain_ref[0:16] = potential[...]
    for copy in upper:
        copy.wait()


def on_device(sizes, bead_charge, bead_cell, bead_count, interp_weights, kernel_fine, kernel_coarse):
    slots = bead_charge.shape[-1]
    charge = bead_charge.reshape(1, slots)
    cells = bead_cell.reshape(1, slots)
    weights = interp_weights.reshape(12, slots)
    vmem = pl.BlockSpec(memory_space=pltpu.VMEM)
    smem = pl.BlockSpec(memory_space=pltpu.SMEM)
    main, tail = pl.pallas_call(
        spread_kernel,
        out_shape=(
            jax.ShapeDtypeStruct((19, 16, LZ), F32),
            jax.ShapeDtypeStruct((3, 24, LZ), F32),
        ),
        in_specs=[smem, vmem, vmem, vmem],
        out_specs=(vmem, vmem),
        scratch_shapes=[pltpu.VMEM((ROWS, LZ), F32)],
        compiler_params=pltpu.CompilerParams(vmem_limit_bytes=40 << 20),
        name="spread",
    )(bead_count, charge, cells, weights)
    dma = pltpu.SemaphoreType.DMA
    pmain, ptail = pl.pallas_call(
        functools.partial(middle_kernel, sizes),
        out_shape=(
            jax.ShapeDtypeStruct((19, 16, LZ), F32),
            jax.ShapeDtypeStruct((3, 24, LZ), F32),
        ),
        in_specs=[vmem] * 4,
        out_specs=(vmem, vmem),
        scratch_shapes=[
            pltpu.VMEM((3, 16, LZ), F32),
            pltpu.VMEM((3, 16, LZ), F32),
            pltpu.VMEM((3, 8, LZ), F32),
            pltpu.VMEM((16, 16, LZ), F32),
            pltpu.VMEM((4, 8, 16, LZ), BF16),
            pltpu.VMEM((4, 4, 16, LZ), BF16),
            pltpu.VMEM((4, 8, 16, LZ), BF16),
            pltpu.VMEM((4, 4, 16, LZ), BF16),
            pltpu.VMEM((32, 32, LZ), F32),
            pltpu.VMEM((SIDE, 32, 16, LZ), BF16),
            pltpu.VMEM((8, 32, LZ), F32),
            pltpu.VMEM((37, 24, LZ), F32),
            pltpu.VMEM((SIDE, SIDE * LZ, LZ), BF16),
            pltpu.VMEM((9, SIDE * LZ, LZ), BF16),
            pltpu.VMEM((4, 8, LZ), F32),
            pltpu.VMEM((8, 4, 8, LZ), F32),
            pltpu.VMEM((12, 24, LZ), F32),
            pltpu.VMEM((SIDE, 12, 8, LZ), F32),
            pltpu.VMEM((256, LZ), F32),
            pltpu.VMEM((4, 8, LZ), F32),
            pltpu.VMEM((8, 4, 8, LZ), F32),
            pltpu.VMEM((6, 24, LZ), F32),
            pltpu.VMEM((16, 24, LZ), F32),
            pltpu.VMEM((3, 16, LZ), F32),
            pltpu.VMEM((16, 16, LZ), F32),
            dma((3,)),
            dma((3,)),
            dma((8,)),
            dma((8,)),
            dma((8,)),
            dma((8,)),
            dma((8,)),
            dma((8,)),
            dma((3,)),
            dma((3,)),
        ],
        compiler_params=pltpu.CompilerParams(
            collective_id=0, has_side_effects=True, vmem_limit_bytes=48 << 20
        ),
        name="middle",
    )(main, tail, kernel_fine, kernel_coarse)
    bead, grid = pl.pallas_call(
        read_kernel,
        out_shape=(
            jax.ShapeDtypeStruct((1, slots), F32),
            jax.ShapeDtypeStruct((16, 16, LZ), F32),
        ),
        in_specs=[smem, vmem, vmem, vmem, vmem],
        out_specs=(vmem, vmem),
        scratch_shapes=[pltpu.VMEM((ROWS, 2 * LZ), BF16)],
        compiler_params=pltpu.CompilerParams(vmem_limit_bytes=40 << 20),
        name="read",
    )(bead_count, cells, weights, pmain, ptail)
    return (bead.reshape(1, 1, slots), grid)


def solution(mesh):
    sizes = (mesh.shape["gx"], mesh.shape["gy"])
    return jax.shard_map(
        functools.partial(on_device, sizes),
        mesh=mesh,
        in_specs=(
            P("gx", "gy", None),
            P("gx", "gy", None),
            P("gx", "gy"),
            P("gx", "gy", None, None),
            P(),
            P(),
        ),
        out_specs=(P("gx", "gy", None), P("gx", "gy", None)),
        check_vma=False,
    )
```

profile of v0, /device:TPU:1, one launch (start us, length us, event | category | flops | bytes accessed | tf_op | source)
XLA Modules:
  0.0 81.6 jit_solution(13430790766512339261)
XLA Ops:
  1.3 0.0 copy-start
  1.3 1.0 %copy-done = bf16[1,1,12,16384]{3,2,1,0:T(8,128)(2,1)S(1)} copy-done((bf16[1,1,12,16384]{3,2,1,0:T(8,128)(2,1)S(1)}, bf16[1,1,12,16384]{3,2,1,0:T(8,128)(2,1)}, u32[]{:S(2)}) %copy-start) | copy-done | bytes 393240
  2.3 0.0 copy-start.2
  2.3 0.8 %copy-done.2 = s32[1,1,16384]{2,1,0:T(1,128)S(1)} copy-done((s32[1,1,16384]{2,1,0:T(1,128)S(1)}, s32[1,1,16384]{2,1,0:T(1,128)}, u32[]{:S(2)}) %copy-start.2) | copy-done | bytes 65560
  3.2 0.0 copy-start.6
  3.2 0.8 %copy-done.6 = f32[1,1,16384]{2,1,0:T(1,128)S(1)} copy-done((f32[1,1,16384]{2,1,0:T(1,128)S(1)}, f32[1,1,16384]{2,1,0:T(1,128)}, u32[]{:S(2)}) %copy-start.6) | copy-done | bytes 65560
  4.0 0.0 copy-start.4
  4.0 0.0 copy-start.1
  4.0 14.9 %spread.1 = (f32[19,16,128]{2,1,0:T(8,128)S(1)}, f32[3,24,128]{2,1,0:T(8,128)S(1)}) custom-call(s32[1,1]{1,0:T(1,128)S(6)} %copy.8.count_ref, f32[1,16384]{1,0:T(1,128)S(1)} %bitcast.8, s32[1,16384]{1,0:T(1,128)S(1)} %bitcast.6, bf16[12,16384]{1,0:T(8,128)(2,1)S(1)} %bitcast.4), custom_call_target="tpu_custom_call" | custom-call | tf_op jit(solution)/shard_map/spread/pallas_call | solution.py:413
  18.9 0.0 copy-done.4
  18.9 0.0 copy-start.5
  18.9 0.9 %copy-done.5 = bf16[17,17,17]{2,1,0:T(8,128)(2,1)S(1)} copy-done((bf16[17,17,17]{2,1,0:T(8,128)(2,1)S(1)}, bf16[17,17,17]{2,1,0:T(8,128)(2,1)}, u32[]{:S(2)}) %copy-start.5) | copy-done | bytes 9850
  19.8 0.0 copy-start.3
  19.8 53.3 %middle.1 = (f32[19,16,128]{2,1,0:T(8,128)S(1)}, f32[3,24,128]{2,1,0:T(8,128)S(1)}) custom-call(f32[19,16,128]{2,1,0:T(8,128)S(1)} %get-tuple-element.8.main_ref, f32[3,24,128]{2,1,0:T(8,128)S(1)} %get-tuple-element.9.tail_ref, bf16[17,17,17]{2,1,0:T(8,128)(2,1)S(1)} %copy-done.4, bf16[17,17,17]{2,1,0:T(8,128)(2,1)S(1)} %copy-done.5), custom_call_target="tpu_custom_call" | custom-call | tf_op jit(solution)/shard_map/middle/pallas_call | solution.py:426
  73.0 0.0 copy-done.1
  73.1 0.0 copy-done.3
  73.1 8.5 %read.1 = (f32[1,16384]{1,0:T(1,128)}, f32[16,16,128]{2,1,0:T(8,128)}) custom-call(s32[1,1]{1,0:T(1,128)S(6)} %copy.8.count_ref, s32[1,16384]{1,0:T(1,128)S(1)} %bitcast.7, bf16[12,16384]{1,0:T(8,128)(2,1)S(1)} %bitcast.5, f32[19,16,128]{2,1,0:T(8,128)S(1)} %get-tuple-element.10.main_ref, f32[3,24,128]{2,1,0:T(8,128)S(1)} %get-tuple-element.11.tail_ref), custom_call_target="tpu_custom_call" | custom-call | tf_op jit(solution)/shard_map/read/pallas_call | solution.py:476
Async XLA Ops:
  1.3 1.0 %copy-start = (bf16[1,1,12,16384]{3,2,1,0:T(8,128)(2,1)S(1)}, bf16[1,1,12,16384]{3,2,1,0:T(8,128)(2,1)}, u32[]{:S(2)}) copy-start(bf16[1,1,12,16384]{3,2,1,0:T(8,128)(2,1)} %param.9) | copy-start | bytes 1179652
  2.3 0.8 %copy-start.2 = (s32[1,1,16384]{2,1,0:T(1,128)S(1)}, s32[1,1,16384]{2,1,0:T(1,128)}, u32[]{:S(2)}) copy-start(s32[1,1,16384]{2,1,0:T(1,128)} %param.7) | copy-start | bytes 196612
  3.2 0.8 %copy-start.6 = (f32[1,1,16384]{2,1,0:T(1,128)S(1)}, f32[1,1,16384]{2,1,0:T(1,128)}, u32[]{:S(2)}) copy-start(f32[1,1,16384]{2,1,0:T(1,128)} %param.6) | copy-start | bytes 196612
  4.0 14.9 %copy-start.4 = (bf16[17,17,17]{2,1,0:T(8,128)(2,1)S(1)}, bf16[17,17,17]{2,1,0:T(8,128)(2,1)}, u32[]{:S(2)}) copy-start(bf16[17,17,17]{2,1,0:T(8,128)(2,1)} %fine_ref.1) | copy-start | bytes 29482
  4.0 69.1 %copy-start.1 = (bf16[1,1,12,16384]{3,2,1,0:T(8,128)(2,1)S(1)}, bf16[1,1,12,16384]{3,2,1,0:T(8,128)(2,1)}, u32[]{:S(2)}) copy-start(bf16[1,1,12,16384]{3,2,1,0:T(8,128)(2,1)} %param.9) | copy-start | bytes 1179652
  18.9 0.9 %copy-start.5 = (bf16[17,17,17]{2,1,0:T(8,128)(2,1)S(1)}, bf16[17,17,17]{2,1,0:T(8,128)(2,1)}, u32[]{:S(2)}) copy-start(bf16[17,17,17]{2,1,0:T(8,128)(2,1)} %coarse_ref.1) | copy-start | bytes 29482
  19.8 53.3 %copy-start.3 = (s32[1,1,16384]{2,1,0:T(1,128)S(1)}, s32[1,1,16384]{2,1,0:T(1,128)}, u32[]{:S(2)}) copy-start(s32[1,1,16384]{2,1,0:T(1,128)} %param.7) | copy-start | bytes 196612
where the time goes:
time: 81.8 us; the launch traced here: 81.6 us
  Pallas kernels  76.6 us (94%)
  local copies, waits for them, and re-layouts  3.61 us (4%)
  between operations  1.33 us (2%)
    pallas_call x1, Pallas kernels, on_device(): pl.pallas_call(functools.partial(middle_kernel, sizes), out_shape=(jax.Sh...  53.3 us
    pallas_call x1, Pallas kernels, on_device(): pl.pallas_call(spread_kernel, out_shape=(jax.ShapeDtypeStruct((19, 16, LZ...  14.9 us
    pallas_call x1, Pallas kernels, on_device(): pl.pallas_call(read_kernel, out_shape=(jax.ShapeDtypeStruct((1, slots), F...  8.49 us
    unnamed x14, local copies, waits for them, and re-layouts  3.61 us

commit v1 on v0

v1 whole, which is shorter than its diff:
```python
import functools

import jax
import jax.numpy as jnp
from jax import lax
from jax.experimental import pallas as pl
from jax.experimental.pallas import tpu as pltpu
from jax.sharding import PartitionSpec as P

LX = 16
LY = 16
LZ = 128
SIDE = 17
BLOCK = 4096
ROWS = 384
STRIP = 1024
GROUP = 5
MESH = pl.DeviceIdType.MESH
F32 = jnp.float32
BF16 = jnp.bfloat16
LANES_BOTH = (((1,), (1,)), ((), ()))
ROWS_BOTH = (((0,), (0,)), ((), ()))
AROUND = [(a, b) for a in (-1, 0, 1) for b in (-1, 0, 1) if (a, b) != (0, 0)]


def iota(shape, dim):
    return lax.broadcasted_iota(jnp.int32, shape, dim)


def split(value):
    high = value.astype(BF16)
    low = (value - high.astype(F32)).astype(BF16)
    return high, low


def bead_tables(cells, weights):
    count = cells.shape[1]
    first = cells >> 11
    second = (cells >> 7) & 15
    third = cells & 127
    rows = iota((24, count), 0)
    away_first = rows - first
    away_second = rows - second
    rows_first = jnp.zeros((24, count), F32)
    rows_second = jnp.zeros((24, count), F32)
    for tap in range(4):
        rows_first = jnp.where(away_first == tap, weights[tap : tap + 1], rows_first)
        rows_second = jnp.where(away_second == tap, weights[4 + tap : 5 + tap], rows_second)
    depth = jnp.zeros((LZ, count), F32)
    away = (iota((LZ, count), 0) - third) & 127
    for tap in range(4):
        depth = jnp.where(away == tap, weights[8 + tap : 9 + tap], depth)
    return rows_first, rows_second, depth.astype(BF16)


def melt_kernel(
    sizes,
    count_ref,
    charge_hbm,
    cell_hbm,
    weight_hbm,
    fine_hbm,
    coarse_hbm,
    bead_ref,
    grid_ref,
    charge_ref,
    cell_ref,
    weight_ref,
    fine_ref,
    coarse_ref,
    load_sem,
    all_first,
    all_second,
    all_depth,
    spread_total,
    main,
    tail,
    side_first,
    side_second,
    side_both,
    charges,
    out_edge,
    out_corner,
    in_edge,
    in_corner,
    grid,
    operand,
    summed,
    lines,
    fine_strips,
    coarse_strips,
    out_coarse,
    in_coarse,
    wide_coarse,
    total,
    own_pot,
    out_pot,
    in_pot,
    wide_pot,
    rows_pot,
    send_tail,
    potential,
    upper_first,
    upper_second,
    upper_both,
    read_table,
    send_1,
    recv_1,
    send_2,
    recv_2,
    send_3,
    recv_3,
    send_4,
    recv_4,
    send_5,
    recv_5,
):
    here_first = lax.axis_index("gx")
    here_second = lax.axis_index("gy")
    live = count_ref[0, 0]

    def device(a, b):
        return (
            lax.rem(here_first + (a + sizes[0]), sizes[0]),
            lax.rem(here_second + (b + sizes[1]), sizes[1]),
        )

    def send(source, target, out_sem, in_sem, a, b):
        copy = pltpu.make_async_remote_copy(
            src_ref=source,
            dst_ref=target,
            send_sem=out_sem,
            recv_sem=in_sem,
            device_id=device(a, b),
            device_id_type=MESH,
        )
        copy.start()
        return copy

    loads = []
    for at, (source, target) in enumerate(
        [
            (cell_hbm, cell_ref),
            (weight_hbm, weight_ref),
            (charge_hbm, charge_ref),
            (fine_hbm, fine_ref),
            (coarse_hbm, coarse_ref),
        ]
    ):
        load = pltpu.make_async_copy(source, target, load_sem.at[at])
        load.start()
        loads.append(load)

    barrier = pltpu.get_barrier_semaphore()
    for a, b in AROUND:
        pl.semaphore_signal(barrier, inc=1, device_id=device(a, b), device_id_type=MESH)

    for load in loads:
        load.wait()

    spread_total[...] = jnp.zeros_like(spread_total)

    def add_block(step, carry):
        start = pl.multiple_of(step * BLOCK, BLOCK)
        here = pl.ds(start, BLOCK)
        slots = iota((1, BLOCK), 1) + start
        charge = jnp.where(slots < live, charge_ref[:, here], 0.0)
        weights = weight_ref[:, here].astype(F32)
        rows_first, rows_second, depth = bead_tables(cell_ref[:, here], weights)
        all_first[:, here] = rows_first
        all_second[:, here] = rows_second
        all_depth[:, here] = depth
        rows_first = rows_first * charge
        parts = [rows_first[x : x + 1] * rows_second[:16] for x in range(19)]
        parts += [rows_second[y : y + 1] * rows_first for y in range(16, 19)]
        parts += [jnp.zeros((8, BLOCK), F32)]
        high, low = split(jnp.concatenate(parts, axis=0))
        spread_total[...] += lax.dot_general(
            high, depth, LANES_BOTH, preferred_element_type=F32
        ) + lax.dot_general(low, depth, LANES_BOTH, preferred_element_type=F32)
        return carry

    lax.fori_loop(0, charge_ref.shape[1] // BLOCK, add_block, 0)
    main[...] = spread_total[0:304].reshape(19, 16, LZ)
    tail[...] = spread_total[304:376].reshape(3, 24, LZ)

    pl.semaphore_wait(barrier, 8)

    spills = [
        send(main.at[16:19], side_first, send_1.at[0], recv_1.at[0], 1, 0),
        send(tail.at[:, 16:24], side_both, send_1.at[2], recv_1.at[2], 1, 1),
        send(tail.at[:, 0:16], side_second, send_1.at[1], recv_1.at[1], 0, 1),
    ]

    lanes = iota((SIDE, LZ), 1)
    taps = iota((SIDE, LZ), 0)
    for at, source in enumerate((fine_ref, coarse_ref)):
        whole = [jnp.zeros((SIDE, LZ), F32)] * 2
        for chunk in range(5):
            placed = jnp.zeros((SIDE, LZ), F32)
            for j in range(4):
                dx = 4 * chunk + j
                if dx < SIDE:
                    place = (lanes == taps + 32 * j).astype(BF16)
                    placed = placed + lax.dot_general(
                        source[dx], place, ROWS_BOTH, preferred_element_type=F32
                    )
            whole.append(placed)
        whole = jnp.concatenate(whole + [jnp.zeros((SIDE, LZ), F32)], axis=1)
        for v in range(4):
            moved = whole if v == 0 else pltpu.roll(whole, STRIP - 32 * v, 1)
            for chunk in range(1, 7):
                lines[at, v, chunk, 0:SIDE] = moved[:, 128 * chunk : 128 * chunk + 128]

    for strips in (fine_strips, coarse_strips):
        strips[:, :, :, 0:128] = jnp.zeros((SIDE, 4, 16, 128), BF16)
        strips[:, :, :, 896:1024] = jnp.zeros((SIDE, 4, 16, 128), BF16)
        strips[:, 0, :, 128:256] = jnp.zeros((SIDE, 16, 128), BF16)
        strips[:, 1:4, :, 768:896] = jnp.zeros((SIDE, 3, 16, 128), BF16)

    def build(dz, carry):
        for at, strips in enumerate((fine_strips, coarse_strips)):
            for v in range(4):
                for chunk in range(2, 7) if v == 0 else range(1, 6):
                    span = slice(128 * chunk, 128 * chunk + 128)
                    line = lines[at, v, chunk, pl.ds(dz, 1)]
                    upper = pltpu.roll(
                        jnp.broadcast_to(line, (8, LZ)), 0, 1, stride=1, stride_axis=0
                    )
                    both = jnp.concatenate([upper, pltpu.roll(upper, 8, 1)], axis=0)
                    strips[dz, v, :, span] = both.astype(BF16)
        return carry

    lax.fori_loop(0, SIDE, build, 0)

    for copy in spills:
        copy.wait()
    charges[...] = main[0:16]
    charges[0:3] += side_first[...]
    for y in range(3):
        side_second[y, 0:8] += side_both[y]
        charges[:, y, :] += side_second[y]
    grid[8:24, 8:24] = charges[...].astype(BF16).astype(F32)

    out_edge[0] = grid[8:16, 8:24].astype(BF16)
    out_edge[1] = grid[16:24, 8:24].astype(BF16)
    out_edge[2] = grid[8:24, 8:16].reshape(8, 16, LZ).astype(BF16)
    out_edge[3] = grid[8:24, 16:24].reshape(8, 16, LZ).astype(BF16)
    for i in range(2):
        for j in range(2):
            quarter = grid[8 + 8 * i : 16 + 8 * i, 8 + 8 * j : 16 + 8 * j]
            out_corner[2 * i + j] = quarter.reshape(4, 16, LZ).astype(BF16)
    halos = []
    for at, (a, b) in enumerate([(-1, 0), (1, 0), (0, -1), (0, 1)]):
        halos.append(send(out_edge.at[at], in_edge.at[at], send_2.at[at], recv_2.at[at], a, b))
    for at, (a, b) in enumerate([(-1, -1), (-1, 1), (1, -1), (1, 1)]):
        halos.append(
            send(out_corner.at[at], in_corner.at[at], send_2.at[4 + at], recv_2.at[4 + at], a, b)
        )
    for copy in halos:
        copy.wait()
    grid[24:32, 8:24] = in_edge[0].astype(F32)
    grid[0:8, 8:24] = in_edge[1].astype(F32)
    grid[8:24, 24:32] = in_edge[2].astype(F32).reshape(16, 8, LZ)
    grid[8:24, 0:8] = in_edge[3].astype(F32).reshape(16, 8, LZ)
    for i in range(2):
        for j in range(2):
            quarter = in_corner[2 * i + j].astype(F32).reshape(8, 8, LZ)
            grid[24 - 24 * i : 32 - 24 * i, 24 - 24 * j : 32 - 24 * j] = quarter

    gap = (iota((LZ, LZ), 0) - 2 * (iota((LZ, LZ), 1) & 63) + 2) & 127
    spline = jnp.where(gap == 2, 0.75, 0.0)
    spline = jnp.where((gap == 1) | (gap == 3), 0.5, spline)
    spline = jnp.where((gap == 0) | (gap == 4), 0.125, spline).astype(BF16)
    coarse_lines = jnp.dot(
        grid[6:25].reshape(19 * 32, LZ).astype(BF16), spline, preferred_element_type=F32
    ).reshape(19, 32, LZ)
    for i in range(8):
        summed[i] = (
            0.125 * (coarse_lines[2 * i] + coarse_lines[2 * i + 4])
            + 0.5 * (coarse_lines[2 * i + 1] + coarse_lines[2 * i + 3])
            + 0.75 * coarse_lines[2 * i + 2]
        )
    lower = iota((8, LZ), 1) < 64
    wide_coarse[:, 24:32] = jnp.zeros((24, 8, LZ), F32)
    planes = []
    for i in range(8):
        parts = [summed[i, pl.ds(6 + t, 8, stride=2)] for t in range(5)]
        plane = 0.125 * (parts[0] + parts[4]) + 0.5 * (parts[1] + parts[3]) + 0.75 * parts[2]
        planes.append(plane.astype(BF16).astype(F32))
    pairs = [jnp.where(lower, planes[2 * j], planes[2 * j + 1]) for j in range(4)]
    for k in range(2):
        out_coarse[k] = jnp.concatenate(pairs[2 * k : 2 * k + 2], axis=0).astype(BF16)
    coarse_sends = []
    for at, (a, b) in enumerate(AROUND):
        coarse_sends.append(send(out_coarse, in_coarse.at[at], send_3.at[at], recv_3.at[at], a, b))
    for i in range(8):
        wide_coarse[8 + i, 8:16] = planes[i]

    def strip_rows(strips, dz):
        columns = []
        for q in range(3):
            blocks = []
            for x in range(8):
                a, v = divmod(8 - x + 8 * q, 4)
                blocks.append(strips[dz, v, :, 128 * a : 128 * a + 256])
            columns.append(jnp.concatenate(blocks, axis=0))
        return jnp.concatenate(columns, axis=1)

    operand[:, 0:LZ] = grid[0:24].reshape(768, LZ).astype(BF16)
    operand[:, LZ:] = grid[8:32].reshape(768, LZ).astype(BF16)
    total[...] = jnp.zeros_like(total)

    def products(strips, right, group):
        rows = jnp.concatenate([strip_rows(strips, dz) for dz in group], axis=0)
        result = jnp.dot(rows, right, preferred_element_type=F32)
        return [result[128 * at : 128 * at + 128] for at in range(len(group))]

    def turned(value, dz):
        return value if dz == 8 else pltpu.roll(value, (136 - dz) % 128, 1)

    def correlate_fine(first, last):
        for start in range(first, last, GROUP):
            group = range(start, min(start + GROUP, last))
            for dz, product in zip(group, products(fine_strips, operand[...], group)):
                total[0] += turned(product[:, :LZ], dz)
                total[1] += turned(product[:, LZ:], dz)

    correlate_fine(0, 9)

    for copy in coarse_sends:
        copy.wait()
    for at, (a, b) in enumerate(AROUND):
        for k in range(2):
            pair_rows = in_coarse[at, k].astype(F32)
            for j in range(2):
                pair = pair_rows[8 * j : 8 * j + 8]
                other = pltpu.roll(pair, 64, 1)
                x = 8 - 8 * a + 4 * k + 2 * j
                wide_coarse[x, 8 - 8 * b : 16 - 8 * b] = jnp.where(lower, pair, other)
                wide_coarse[x + 1, 8 - 8 * b : 16 - 8 * b] = jnp.where(lower, other, pair)
    coarse_operand = wide_coarse[...].reshape(768, LZ).astype(BF16)
    own_pot[...] = jnp.zeros_like(own_pot)

    for start in range(0, SIDE, GROUP):
        group = range(start, min(start + GROUP, SIDE))
        for dz, product in zip(group, products(coarse_strips, coarse_operand, group)):
            near = product.reshape(8, 16, LZ)[:, 0:8].reshape(64, LZ)
            own_pot[...] += turned(near, dz).reshape(8, 8, LZ)

    out_pot[0] = own_pot[:, 0, :]
    out_pot[1] = own_pot[:, 7, :]
    pot_sends = []
    for at, (a, b) in enumerate(AROUND):
        if a == 0:
            source = out_pot.at[0 if b < 0 else 1]
        else:
            source = own_pot.at[0 if a < 0 else 7]
        pot_sends.append(send(source, in_pot.at[at], send_4.at[at], recv_4.at[at], a, b))

    correlate_fine(9, SIDE)

    for copy in pot_sends:
        copy.wait()
    wide_pot[1:9, 8:16] = own_pot[...]
    for at, (a, b) in enumerate(AROUND):
        if a == 0:
            wide_pot[1:9, 16 if b < 0 else 7, :] = in_pot[at]
        else:
            wide_pot[9 if a < 0 else 0, 8 - 8 * b : 16 - 8 * b] = in_pot[at]
    for i in range(8):
        rows_pot[2 * i] = (wide_pot[i] + 6.0 * wide_pot[i + 1] + wide_pot[i + 2]) * 0.125
        rows_pot[2 * i + 1] = (wide_pot[i + 1] + wide_pot[i + 2]) * 0.5
    below = rows_pot[:, 7:15]
    middle = rows_pot[:, 8:16]
    above = rows_pot[:, 9:17]
    even_rows = (below + 6.0 * middle + above) * 0.125
    odd_rows = (middle + above) * 0.5
    for i in range(16):
        potential[i, pl.ds(0, 8, stride=2)] = even_rows[i]
        potential[i, pl.ds(1, 8, stride=2)] = odd_rows[i]
    source = iota((LZ, LZ), 0)
    offset = (iota((LZ, LZ), 1) - 2 * source + 2) & 127
    refine = jnp.where(offset == 2, 0.75, 0.0)
    refine = jnp.where((offset == 1) | (offset == 3), 0.5, refine)
    refine = jnp.where((offset == 0) | (offset == 4), 0.125, refine)
    refine = jnp.where(source < 64, refine, 0.0).astype(BF16)
    high, low = split(potential[...].reshape(256, LZ))
    smooth = jnp.dot(
        jnp.concatenate([high, low], axis=1),
        jnp.concatenate([refine, refine], axis=0),
        preferred_element_type=F32,
    )
    potential[...] = (total[...].reshape(256, LZ) + smooth).reshape(16, 16, LZ)

    for y in range(3):
        send_tail[y] = potential[:, y, :]
    upper = [
        send(potential.at[0:3], upper_first, send_5.at[0], recv_5.at[0], -1, 0),
        send(send_tail.at[:, 0:8], upper_both, send_5.at[2], recv_5.at[2], -1, -1),
        send(send_tail, upper_second, send_5.at[1], recv_5.at[1], 0, -1),
    ]
    grid_ref[...] = potential[...]

    def put_table(start, rows):
        high, low = split(rows)
        read_table[start : start + rows.shape[0], 0:LZ] = high
        read_table[start : start + rows.shape[0], LZ:] = low

    put_table(0, potential[...].reshape(256, LZ))
    for copy in upper:
        copy.wait()
    put_table(256, upper_first[...].reshape(48, LZ))
    ends = []
    for y in range(3):
        ends += [upper_second[y], upper_both[y]]
    ends += [jnp.zeros((8, LZ), F32)]
    put_table(304, jnp.concatenate(ends, axis=0))

    def read_block(step, carry):
        start = pl.multiple_of(step * BLOCK, BLOCK)
        here = pl.ds(start, BLOCK)
        rows_first = all_first[:, here]
        rows_second = all_second[:, here]
        depth = all_depth[:, here]
        along = jnp.dot(
            read_table[...], jnp.concatenate([depth, depth], axis=0), preferred_element_type=F32
        )
        near = jnp.zeros((16, BLOCK), F32)
        for x in range(19):
            near = near + rows_first[x : x + 1] * along[16 * x : 16 * x + 16]
        far = jnp.zeros((24, BLOCK), F32)
        for y in range(3):
            far = far + rows_second[16 + y : 17 + y] * along[304 + 24 * y : 328 + 24 * y]
        near = near * rows_second[:16]
        far = far * rows_first
        both = near[:8] + near[8:] + far[:8] + far[8:16] + far[16:]
        slots = iota((1, BLOCK), 1) + start
        value = jnp.sum(both, axis=0, keepdims=True)
        bead_ref[:, here] = jnp.where(slots < live, value, 0.0)
        return carry

    lax.fori_loop(0, cell_ref.shape[1] // BLOCK, read_block, 0)


def on_device(sizes, bead_charge, bead_cell, bead_count, interp_weights, kernel_fine, kernel_coarse):
    slots = bead_charge.shape[-1]
    charge = bead_charge.reshape(1, slots)
    cells = bead_cell.reshape(1, slots)
    weights = interp_weights.reshape(12, slots)
    vmem = pl.BlockSpec(memory_space=pltpu.VMEM)
    smem = pl.BlockSpec(memory_space=pltpu.SMEM)
    anywhere = pl.BlockSpec(memory_space=pl.ANY)
    dma = pltpu.SemaphoreType.DMA
    scratch = [
        pltpu.VMEM((1, slots), F32),
        pltpu.VMEM((1, slots), jnp.int32),
        pltpu.VMEM((12, slots), BF16),
        pltpu.VMEM((SIDE, SIDE, SIDE), BF16),
        pltpu.VMEM((SIDE, SIDE, SIDE), BF16),
        dma((5,)),
        pltpu.VMEM((24, slots), F32),
        pltpu.VMEM((24, slots), F32),
        pltpu.VMEM((LZ, slots), BF16),
        pltpu.VMEM((ROWS, LZ), F32),
        pltpu.VMEM((19, 16, LZ), F32),
        pltpu.VMEM((3, 24, LZ), F32),
        pltpu.VMEM((3, 16, LZ), F32),
        pltpu.VMEM((3, 16, LZ), F32),
        pltpu.VMEM((3, 8, LZ), F32),
        pltpu.VMEM((16, 16, LZ), F32),
        pltpu.VMEM((4, 8, 16, LZ), BF16),
        pltpu.VMEM((4, 4, 16, LZ), BF16),
        pltpu.VMEM((4, 8, 16, LZ), BF16),
        pltpu.VMEM((4, 4, 16, LZ), BF16),
        pltpu.VMEM((32, 32, LZ), F32),
        pltpu.VMEM((768, 2 * LZ), BF16),
        pltpu.VMEM((8, 32, LZ), F32),
        pltpu.VMEM((2, 4, 8, 24, LZ), F32),
        pltpu.VMEM((SIDE, 4, 16, STRIP), BF16),
        pltpu.VMEM((SIDE, 4, 16, STRIP), BF16),
        pltpu.VMEM((2, 16, LZ), BF16),
        pltpu.VMEM((8, 2, 16, LZ), BF16),
        pltpu.VMEM((24, 32, LZ), F32),
        pltpu.VMEM((2, LZ, LZ), F32),
        pltpu.VMEM((8, 8, LZ), F32),
        pltpu.VMEM((2, 8, LZ), F32),
        pltpu.VMEM((8, 8, LZ), F32),
        pltpu.VMEM((10, 24, LZ), F32),
        pltpu.VMEM((16, 24, LZ), F32),
        pltpu.VMEM((3, 16, LZ), F32),
        pltpu.VMEM((16, 16, LZ), F32),
        pltpu.VMEM((3, 16, LZ), F32),
        pltpu.VMEM((3, 16, LZ), F32),
        pltpu.VMEM((3, 8, LZ), F32),
        pltpu.VMEM((ROWS, 2 * LZ), BF16),
    ]
    for count in (3, 8, 8, 8, 3):
        scratch += [dma((count,)), dma((count,))]
    bead, grid = pl.pallas_call(
        functools.partial(melt_kernel, sizes),
        out_shape=(
            jax.ShapeDtypeStruct((1, slots), F32),
            jax.ShapeDtypeStruct((16, 16, LZ), F32),
        ),
        in_specs=[smem] + [anywhere] * 5,
        out_specs=(vmem, vmem),
        scratch_shapes=scratch,
        compiler_params=pltpu.CompilerParams(
            collective_id=0, has_side_effects=True, vmem_limit_bytes=60 << 20
        ),
        name="melt",
    )(bead_count, charge, cells, weights, kernel_fine, kernel_coarse)
    return (bead.reshape(1, 1, slots), grid)


def solution(mesh):
    sizes = (mesh.shape["gx"], mesh.shape["gy"])
    return jax.shard_map(
        functools.partial(on_device, sizes),
        mesh=mesh,
        in_specs=(
            P("gx", "gy", None),
            P("gx", "gy", None),
            P("gx", "gy"),
            P("gx", "gy", None, None),
            P(),
            P(),
        ),
        out_specs=(P("gx", "gy", None), P("gx", "gy", None)),
        check_vma=False,
    )
```

time: 81.8 us -> 63 us (0.77)
  Pallas kernels: 76.6 us -> 59.4 us
  local copies, waits for them, and re-layouts: 3.61 us -> 2.17 us
    pallas_call x3 -> x1, Pallas kernels: 76.6 us -> 59.4 us  [on_device(): pl.pallas_call(functools.partial(melt_kernel, sizes), out_shape=(jax.Shap...]
    unnamed x14 -> x4, local copies, waits for them, and re-layouts: 3.61 us -> 2.17 us
where the time goes in v1:
time: 63 us; the launch traced here: 62.8 us
  Pallas kernels  59.4 us (94%)
  local copies, waits for them, and re-layouts  2.17 us (3%)
  between operations  1.29 us (2%)
    pallas_call x1, Pallas kernels, on_device(): pl.pallas_call(functools.partial(melt_kernel, sizes), out_shape=(jax.Shap...  59.4 us
    unnamed x4, local copies, waits for them, and re-layouts  2.17 us

profile of v1, /device:TPU:1, one launch (start us, length us, event | category | flops | bytes accessed | tf_op | source)
XLA Modules:
  0.0 62.8 jit_solution(3063340898848506556)
XLA Ops:
  1.3 59.4 %melt.1 = (f32[1,16384]{1,0:T(1,128)}, f32[16,16,128]{2,1,0:T(8,128)}) custom-call(s32[1,1]{1,0:T(1,128)S(6)} %copy.10.count_ref, f32[1,16384]{1,0:T(1,128)} %bitcast.5, s32[1,16384]{1,0:T(1,128)} %bitcast.6, bf16[12,16384]{1,0:T(8,128)(2,1)} %bitcast.4, bf16[17,17,17]{2,1,0:T(8,128)(2,1)} %fine_hbm.1, bf16[17,17,17]{2,1,0:T(8,128)(2,1)} %coarse_hbm.1), custom_call_target="tpu_custom_call" | custom-call | tf_op jit(solution)/shard_map/melt/pallas_call | solution.py:500
  60.7 0.0 copy-start
  60.7 1.5 %copy.11 = f32[1,1,16384]{2,1,0:T(1,128)} copy(f32[1,1,16384]{2,1,0:T(1,128)} %bitcast.7) | data formatting | bytes 131072
  62.2 0.0 copy-done
  62.2 0.7 %copy.12 = f32[16,16,128]{2,1,0:T(8,128)} copy(f32[16,16,128]{2,1,0:T(8,128)S(1)} %copy-done) | data formatting | bytes 262144
Async XLA Ops:
  60.7 1.5 %copy-start = (f32[16,16,128]{2,1,0:T(8,128)S(1)}, f32[16,16,128]{2,1,0:T(8,128)}, u32[]{:S(2)}) copy-start(f32[16,16,128]{2,1,0:T(8,128)} %get-tuple-element.9) | copy-start | bytes 393220

commit v2 on v1

--- a/solution.py
+++ b/solution.py
@@ -11,7 +11,7 @@
 LY = 16
 LZ = 128
 SIDE = 17
-BLOCK = 4096
+BLOCK = 8192
 ROWS = 384
 STRIP = 1024
 GROUP = 5
@@ -46,11 +46,12 @@
     for tap in range(4):
         rows_first = jnp.where(away_first == tap, weights[tap : tap + 1], rows_first)
         rows_second = jnp.where(away_second == tap, weights[4 + tap : 5 + tap], rows_second)
-    depth = jnp.zeros((LZ, count), F32)
-    away = (iota((LZ, count), 0) - third) & 127
+    depth = jnp.zeros((LZ, count), BF16)
+    places = iota((LZ, count), 0).astype(F32).astype(BF16)
     for tap in range(4):
-        depth = jnp.where(away == tap, weights[8 + tap : 9 + tap], depth)
-    return rows_first, rows_second, depth.astype(BF16)
+        target = ((third + tap) & 127).astype(F32).astype(BF16)
+        depth = jnp.where(places == target, weights[8 + tap : 9 + tap].astype(BF16), depth)
+    return rows_first, rows_second, depth
 
 
 def melt_kernel(
@@ -72,8 +73,9 @@
     all_first,
     all_second,
     all_depth,
-    spread_total,
-    main,
+    far_total,
+    near_total,
+    main_far,
     tail,
     side_first,
     side_second,
@@ -158,40 +160,81 @@
     for load in loads:
         load.wait()
 
-    spread_total[...] = jnp.zeros_like(spread_total)
-
-    def add_block(step, carry):
+    far_total[...] = jnp.zeros_like(far_total)
+    near_total[...] = jnp.zeros_like(near_total)
+
+    def block_at(step):
         start = pl.multiple_of(step * BLOCK, BLOCK)
-        here = pl.ds(start, BLOCK)
-        slots = iota((1, BLOCK), 1) + start
-        charge = jnp.where(slots < live, charge_ref[:, here], 0.0)
+        return pl.ds(start, BLOCK), iota((1, BLOCK), 1) + start < live
+
+    def add_rows(sums, parts, depth):
+        high, low = split(jnp.concatenate(parts, axis=0))
+        both = lax.dot_general(
+            jnp.concatenate([high, low], axis=0), depth, LANES_BOTH, preferred_element_type=F32
+        )
+        sums[...] += both[: high.shape[0]] + both[high.shape[0] :]
+
+    def spread_far(step, carry):
+        here, alive = block_at(step)
         weights = weight_ref[:, here].astype(F32)
         rows_first, rows_second, depth = bead_tables(cell_ref[:, here], weights)
         all_first[:, here] = rows_first
         all_second[:, here] = rows_second
         all_depth[:, here] = depth
-        rows_first = rows_first * charge
-        parts = [rows_first[x : x + 1] * rows_second[:16] for x in range(19)]
+        rows_first = rows_first * jnp.where(alive, charge_ref[:, here], 0.0)
+        parts = [rows_first[x : x + 1] * rows_second[:16] for x in range(16, 19)]
         parts += [rows_second[y : y + 1] * rows_first for y in range(16, 19)]
         parts += [jnp.zeros((8, BLOCK), F32)]
-        high, low = split(jnp.concatenate(parts, axis=0))
-        spread_total[...] += lax.dot_general(
-            high, depth, LANES_BOTH, preferred_element_type=F32
-        ) + lax.dot_general(low, depth, LANES_BOTH, preferred_element_type=F32)
+        add_rows(far_total, parts, depth)
         return carry
 
-    lax.fori_loop(0, charge_ref.shape[1] // BLOCK, add_block, 0)
-    main[...] = spread_total[0:304].reshape(19, 16, LZ)
-    tail[...] = spread_total[304:376].reshape(3, 24, LZ)
+    def spread_near(step, carry):
+        here, alive = block_at(step)
+        rows_first = all_first[0:16, here] * jnp.where(alive, charge_ref[:, here], 0.0)
+        rows_second = all_second[0:16, here]
+        parts = [rows_first[x : x + 1] * rows_second for x in range(16)]
+        add_rows(near_total, parts, all_depth[:, here])
+        return carry
+
+    steps = charge_ref.shape[1] // BLOCK
+    lax.fori_loop(0, steps, spread_far, 0)
+    main_far[...] = far_total[0:48].reshape(3, 16, LZ)
+    tail[...] = far_total[48:120].reshape(3, 24, LZ)
 
     pl.semaphore_wait(barrier, 8)
 
     spills = [
-        send(main.at[16:19], side_first, send_1.at[0], recv_1.at[0], 1, 0),
+        send(main_far, side_first, send_1.at[0], recv_1.at[0], 1, 0),
         send(tail.at[:, 16:24], side_both, send_1.at[2], recv_1.at[2], 1, 1),
         send(tail.at[:, 0:16], side_second, send_1.at[1], recv_1.at[1], 0, 1),
     ]
 
+    lax.fori_loop(0, steps, spread_near, 0)
+
+    for copy in spills:
+        copy.wait()
+    charges[...] = near_total[...].reshape(16, 16, LZ)
+    charges[0:3] += side_first[...]
+    for y in range(3):
+        side_second[y, 0:8] += side_both[y]
+        charges[:, y, :] += side_second[y]
+    grid[8:24, 8:24] = charges[...].astype(BF16).astype(F32)
+
+    out_edge[0] = grid[8:16, 8:24].astype(BF16)
+    out_edge[1] = grid[16:24, 8:24].astype(BF16)
+    out_edge[2] = grid[8:24, 8:16].reshape(8, 16, LZ).astype(BF16)
+    out_edge[3] = grid[8:24, 16:24].reshape(8, 16, LZ).astype(BF16)
+    for i in range(2):
+        for j in range(2):
+            quarter = grid[8 + 8 * i : 16 + 8 * i, 8 + 8 * j : 16 + 8 * j]
+            out_corner[2 * i + j] = quarter.reshape(4, 16, LZ).astype(BF16)
+    halos = []
+    for at, (a, b) in enumerate([(-1, 0), (1, 0), (0, -1), (0, 1)]):
+        halos.append(send(out_edge.at[at], in_edge.at[at], send_2.at[at], recv_2.at[at], a, b))
+    for at, (a, b) in enumerate([(-1, -1), (-1, 1), (1, -1), (1, 1)]):
+        halos.append(
+            send(out_corner.at[at], in_corner.at[at], send_2.at[4 + at], recv_2.at[4 + at], a, b)
+        )
     lanes = iota((SIDE, LZ), 1)
     taps = iota((SIDE, LZ), 0)
     for at, source in enumerate((fine_ref, coarse_ref)):
@@ -233,30 +276,6 @@
 
     lax.fori_loop(0, SIDE, build, 0)
 
-    for copy in spills:
-        copy.wait()
-    charges[...] = main[0:16]
-    charges[0:3] += side_first[...]
-    for y in range(3):
-        side_second[y, 0:8] += side_both[y]
-        charges[:, y, :] += side_second[y]
-    grid[8:24, 8:24] = charges[...].astype(BF16).astype(F32)
-
-    out_edge[0] = grid[8:16, 8:24].astype(BF16)
-    out_edge[1] = grid[16:24, 8:24].astype(BF16)
-    out_edge[2] = grid[8:24, 8:16].reshape(8, 16, LZ).astype(BF16)
-    out_edge[3] = grid[8:24, 16:24].reshape(8, 16, LZ).astype(BF16)
-    for i in range(2):
-        for j in range(2):
-            quarter = grid[8 + 8 * i : 16 + 8 * i, 8 + 8 * j : 16 + 8 * j]
-            out_corner[2 * i + j] = quarter.reshape(4, 16, LZ).astype(BF16)
-    halos = []
-    for at, (a, b) in enumerate([(-1, 0), (1, 0), (0, -1), (0, 1)]):
-        halos.append(send(out_edge.at[at], in_edge.at[at], send_2.at[at], recv_2.at[at], a, b))
-    for at, (a, b) in enumerate([(-1, -1), (-1, 1), (1, -1), (1, 1)]):
-        halos.append(
-            send(out_corner.at[at], in_corner.at[at], send_2.at[4 + at], recv_2.at[4 + at], a, b)
-        )
     for copy in halos:
         copy.wait()
     grid[24:32, 8:24] = in_edge[0].astype(F32)
@@ -408,6 +427,23 @@
         read_table[start : start + rows.shape[0], LZ:] = low
 
     put_table(0, potential[...].reshape(256, LZ))
+
+    def read_near(step, carry):
+        here, _ = block_at(step)
+        depth = all_depth[:, here]
+        along = jnp.dot(
+            read_table[0:256], jnp.concatenate([depth, depth], axis=0), preferred_element_type=F32
+        )
+        rows_first = all_first[:, here]
+        near = jnp.zeros((16, BLOCK), F32)
+        for x in range(16):
+            near = near + rows_first[x : x + 1] * along[16 * x : 16 * x + 16]
+        near = near * all_second[0:16, here]
+        bead_ref[:, here] = jnp.sum(near[:8] + near[8:], axis=0, keepdims=True)
+        return carry
+
+    lax.fori_loop(0, steps, read_near, 0)
+
     for copy in upper:
         copy.wait()
     put_table(256, upper_first[...].reshape(48, LZ))
@@ -417,30 +453,35 @@
     ends += [jnp.zeros((8, LZ), F32)]
     put_table(304, jnp.concatenate(ends, axis=0))
 
-    def read_block(step, carry):
-        start = pl.multiple_of(step * BLOCK, BLOCK)
-        here = pl.ds(start, BLOCK)
+    def read_far(step, carry):
+        here, alive = block_at(step)
+        depth = all_depth[:, here]
+        along = jnp.dot(
+            read_table[256:384],
+            jnp.concatenate([depth, depth], axis=0),
+            preferred_element_type=F32,
+        )
         rows_first = all_first[:, here]
         rows_second = all_second[:, here]
-        depth = all_depth[:, here]
-        along = jnp.dot(
-            read_table[...], jnp.concatenate([depth, depth], axis=0), preferred_element_type=F32
-        )
         near = jnp.zeros((16, BLOCK), F32)
-        for x in range(19):
-            near = near + rows_first[x : x + 1] * along[16 * x : 16 * x + 16]
+        for x in range(3):
+            near = near + rows_first[16 + x : 17 + x] * along[16 * x : 16 * x + 16]
         far = jnp.zeros((24, BLOCK), F32)
         for y in range(3):
-            far = far + rows_second[16 + y : 17 + y] * along[304 + 24 * y : 328 + 24 * y]
+            far = far + rows_second[16 + y : 17 + y] * along[48 + 24 * y : 72 + 24 * y]
         near = near * rows_second[:16]
         far = far * rows_first
         both = near[:8] + near[8:] + far[:8] + far[8:16] + far[16:]
-        slots = iota((1, BLOCK), 1) + start
-        value = jnp.sum(both, axis=0, keepdims=True)
-        bead_ref[:, here] = jnp.where(slots < live, value, 0.0)
+        value = bead_ref[:, here] + jnp.sum(both, axis=0, keepdims=True)
+        bead_ref[:, here] = jnp.where(alive, value, 0.0)
         return carry
 
-    lax.fori_loop(0, cell_ref.shape[1] // BLOCK, read_block, 0)
+    lax.fori_loop(0, steps, read_far, 0)
+
+
+def hand_over(bead_from, grid_from, bead_to, grid_to):
+    bead_to[...] = bead_from[...]
+    grid_to[...] = grid_from[...]
 
 
 def on_device(sizes, bead_charge, bead_cell, bead_count, interp_weights, kernel_fine, kernel_coarse):
@@ -462,8 +503,9 @@
         pltpu.VMEM((24, slots), F32),
         pltpu.VMEM((24, slots), F32),
         pltpu.VMEM((LZ, slots), BF16),
-        pltpu.VMEM((ROWS, LZ), F32),
-        pltpu.VMEM((19, 16, LZ), F32),
+        pltpu.VMEM((128, LZ), F32),
+        pltpu.VMEM((256, LZ), F32),
+        pltpu.VMEM((3, 16, LZ), F32),
         pltpu.VMEM((3, 24, LZ), F32),
         pltpu.VMEM((3, 16, LZ), F32),
         pltpu.VMEM((3, 16, LZ), F32),
@@ -511,6 +553,16 @@
         ),
         name="melt",
     )(bead_count, charge, cells, weights, kernel_fine, kernel_coarse)
+    bead, grid = pl.pallas_call(
+        hand_over,
+        out_shape=(
+            jax.ShapeDtypeStruct((1, slots), F32),
+            jax.ShapeDtypeStruct((16, 16, LZ), F32),
+        ),
+        in_specs=[vmem, vmem],
+        out_specs=(vmem, vmem),
+        name="hand_over",
+    )(bead, grid)
     return (bead.reshape(1, 1, slots), grid)
 
 

time: 63 us -> 52.6 us (0.83)
  Pallas kernels: 59.4 us -> 51.2 us
  local copies, waits for them, and re-layouts: 2.17 us -> 0 us
    pallas_call x1, Pallas kernels: 59.4 us -> 49.6 us  [on_device(): pl.pallas_call(functools.partial(melt_kernel, sizes), out_shape=(jax.Shap...]
    unnamed x4 -> x0, local copies, waits for them, and re-layouts: 2.17 us -> none
    pallas_call x0 -> x1, Pallas kernels: none -> 1.63 us  [on_device(): pl.pallas_call(hand_over, out_shape=(jax.ShapeDtypeStruct((1, slots), F32...]
where the time goes in v2:
time: 52.6 us; the launch traced here: 52.5 us
  Pallas kernels  51.2 us (97%)
  between operations  1.28 us (2%)
    pallas_call x1, Pallas kernels, on_device(): pl.pallas_call(functools.partial(melt_kernel, sizes), out_shape=(jax.Shap...  49.6 us
    pallas_call x1, Pallas kernels, on_device(): pl.pallas_call(hand_over, out_shape=(jax.ShapeDtypeStruct((1, slots), F32...  1.63 us

profile of v2, /device:TPU:1, one launch (start us, length us, event | category | flops | bytes accessed | tf_op | source)
XLA Modules:
  0.0 52.5 jit_solution(12882599669669995538)
XLA Ops:
  1.3 49.6 %melt.1 = (f32[1,16384]{1,0:T(1,128)}, f32[16,16,128]{2,1,0:T(8,128)}) custom-call(s32[1,1]{1,0:T(1,128)S(6)} %copy.8.count_ref, f32[1,16384]{1,0:T(1,128)} %bitcast.5, s32[1,16384]{1,0:T(1,128)} %bitcast.6, bf16[12,16384]{1,0:T(8,128)(2,1)} %bitcast.4, bf16[17,17,17]{2,1,0:T(8,128)(2,1)} %fine_hbm.1, bf16[17,17,17]{2,1,0:T(8,128)(2,1)} %coarse_hbm.1), custom_call_target="tpu_custom_call" | custom-call | tf_op jit(solution)/shard_map/melt/pallas_call | solution.py:542
  50.8 1.6 %hand_over.1 = (f32[1,16384]{1,0:T(1,128)}, f32[16,16,128]{2,1,0:T(8,128)}) custom-call(f32[1,16384]{1,0:T(1,128)} %get-tuple-element.6.bead_from, f32[16,16,128]{2,1,0:T(8,128)} %get-tuple-element.7.grid_from), custom_call_target="tpu_custom_call" | custom-call | tf_op jit(solution)/shard_map/hand_over/pallas_call | solution.py:556

commit v3 on v2

--- a/solution.py
+++ b/solution.py
@@ -91,13 +91,11 @@
     lines,
     fine_strips,
     coarse_strips,
+    own_coarse,
     out_coarse,
     in_coarse,
     wide_coarse,
     total,
-    own_pot,
-    out_pot,
-    in_pot,
     wide_pot,
     rows_pot,
     send_tail,
@@ -112,8 +110,6 @@
     recv_2,
     send_3,
     recv_3,
-    send_4,
-    recv_4,
     send_5,
     recv_5,
 ):
@@ -275,6 +271,7 @@
         return carry
 
     lax.fori_loop(0, SIDE, build, 0)
+    wide_coarse[...] = jnp.zeros_like(wide_coarse)
 
     for copy in halos:
         copy.wait()
@@ -292,29 +289,37 @@
     spline = jnp.where((gap == 1) | (gap == 3), 0.5, spline)
     spline = jnp.where((gap == 0) | (gap == 4), 0.125, spline).astype(BF16)
     coarse_lines = jnp.dot(
-        grid[6:25].reshape(19 * 32, LZ).astype(BF16), spline, preferred_element_type=F32
-    ).reshape(19, 32, LZ)
-    for i in range(8):
+        grid[4:27].reshape(23 * 32, LZ).astype(BF16), spline, preferred_element_type=F32
+    ).reshape(23, 32, LZ)
+    for i in range(10):
         summed[i] = (
             0.125 * (coarse_lines[2 * i] + coarse_lines[2 * i + 4])
             + 0.5 * (coarse_lines[2 * i + 1] + coarse_lines[2 * i + 3])
             + 0.75 * coarse_lines[2 * i + 2]
         )
+    for i in range(10):
+        parts = [summed[i, pl.ds(4 + t, 10, stride=2)] for t in range(5)]
+        plane = 0.125 * (parts[0] + parts[4]) + 0.5 * (parts[1] + parts[3]) + 0.75 * parts[2]
+        own_coarse[i, 0:10] = plane.astype(BF16).astype(F32)
     lower = iota((8, LZ), 1) < 64
-    wide_coarse[:, 24:32] = jnp.zeros((24, 8, LZ), F32)
-    planes = []
-    for i in range(8):
-        parts = [summed[i, pl.ds(6 + t, 8, stride=2)] for t in range(5)]
-        plane = 0.125 * (parts[0] + parts[4]) + 0.5 * (parts[1] + parts[3]) + 0.75 * parts[2]
-        planes.append(plane.astype(BF16).astype(F32))
-    pairs = [jnp.where(lower, planes[2 * j], planes[2 * j + 1]) for j in range(4)]
-    for k in range(2):
-        out_coarse[k] = jnp.concatenate(pairs[2 * k : 2 * k + 2], axis=0).astype(BF16)
+    inner = [own_coarse[1 + i, 1:9] for i in range(8)]
+    pairs = [jnp.where(lower, inner[2 * j], inner[2 * j + 1]) for j in range(4)]
+    mains = [jnp.concatenate(pairs[2 * k : 2 * k + 2], axis=0).astype(BF16) for k in range(2)]
+    columns = {1: own_coarse[1:9, 0, :], -1: own_coarse[1:9, 9, :], 0: inner[0]}
     coarse_sends = []
     for at, (a, b) in enumerate(AROUND):
-        coarse_sends.append(send(out_coarse, in_coarse.at[at], send_3.at[at], recv_3.at[at], a, b))
+        x = 0 if a > 0 else 9
+        y = 0 if b > 0 else 9
+        outer = jnp.where(lower, own_coarse[x, 1:9], columns[b])
+        corner = jnp.broadcast_to(own_coarse[x, y : y + 1], (8, LZ))
+        out_coarse[at, 0] = mains[0]
+        out_coarse[at, 1] = mains[1]
+        out_coarse[at, 2] = jnp.concatenate([outer, corner], axis=0).astype(BF16)
+        coarse_sends.append(
+            send(out_coarse.at[at], in_coarse.at[at], send_3.at[at], recv_3.at[at], a, b)
+        )
     for i in range(8):
-        wide_coarse[8 + i, 8:16] = planes[i]
+        wide_coarse[9 + i, 9:17] = inner[i]
 
     def strip_rows(strips, dz):
         columns = []
@@ -345,54 +350,47 @@
                 total[0] += turned(product[:, :LZ], dz)
                 total[1] += turned(product[:, LZ:], dz)
 
-    correlate_fine(0, 9)
+    correlate_fine(0, SIDE)
 
     for copy in coarse_sends:
         copy.wait()
     for at, (a, b) in enumerate(AROUND):
+        x, y = 9 - 8 * a, 9 - 8 * b
         for k in range(2):
             pair_rows = in_coarse[at, k].astype(F32)
             for j in range(2):
                 pair = pair_rows[8 * j : 8 * j + 8]
                 other = pltpu.roll(pair, 64, 1)
-                x = 8 - 8 * a + 4 * k + 2 * j
-                wide_coarse[x, 8 - 8 * b : 16 - 8 * b] = jnp.where(lower, pair, other)
-                wide_coarse[x + 1, 8 - 8 * b : 16 - 8 * b] = jnp.where(lower, other, pair)
-    coarse_operand = wide_coarse[...].reshape(768, LZ).astype(BF16)
-    own_pot[...] = jnp.zeros_like(own_pot)
+                place = x + 4 * k + 2 * j
+                wide_coarse[place, y : y + 8] = jnp.where(lower, pair, other)
+                wide_coarse[place + 1, y : y + 8] = jnp.where(lower, other, pair)
+        outer_rows = in_coarse[at, 2].astype(F32)
+        outer = outer_rows[0:8]
+        other = pltpu.roll(outer, 64, 1)
+        x_outer = 0 if a > 0 else 25
+        y_outer = 0 if b > 0 else 25
+        if a != 0:
+            wide_coarse[x_outer, y : y + 8] = jnp.where(lower, outer, other)
+        if b != 0:
+            wide_coarse[x : x + 8, y_outer, :] = jnp.where(lower, other, outer)
+        if a != 0 and b != 0:
+            wide_coarse[x_outer, y_outer : y_outer + 1] = outer_rows[8:9]
+    operand[:, 0:LZ] = wide_coarse[0:24].reshape(768, LZ).astype(BF16)
+    operand[:, LZ:] = wide_coarse[8:32].reshape(768, LZ).astype(BF16)
+    wide_pot[...] = jnp.zeros_like(wide_pot)
 
     for start in range(0, SIDE, GROUP):
         group = range(start, min(start + GROUP, SIDE))
-        for dz, product in zip(group, products(coarse_strips, coarse_operand, group)):
-            near = product.reshape(8, 16, LZ)[:, 0:8].reshape(64, LZ)
-            own_pot[...] += turned(near, dz).reshape(8, 8, LZ)
-
-    out_pot[0] = own_pot[:, 0, :]
-    out_pot[1] = own_pot[:, 7, :]
-    pot_sends = []
-    for at, (a, b) in enumerate(AROUND):
-        if a == 0:
-            source = out_pot.at[0 if b < 0 else 1]
-        else:
-            source = own_pot.at[0 if a < 0 else 7]
-        pot_sends.append(send(source, in_pot.at[at], send_4.at[at], recv_4.at[at], a, b))
-
-    correlate_fine(9, SIDE)
-
-    for copy in pot_sends:
-        copy.wait()
-    wide_pot[1:9, 8:16] = own_pot[...]
-    for at, (a, b) in enumerate(AROUND):
-        if a == 0:
-            wide_pot[1:9, 16 if b < 0 else 7, :] = in_pot[at]
-        else:
-            wide_pot[9 if a < 0 else 0, 8 - 8 * b : 16 - 8 * b] = in_pot[at]
+        for dz, product in zip(group, products(coarse_strips, operand[...], group)):
+            wide_pot[0:8] += turned(product[:, :LZ], dz).reshape(8, 16, LZ)
+            wide_pot[8:10] += turned(product[0:32, LZ:], dz).reshape(2, 16, LZ)
+
     for i in range(8):
         rows_pot[2 * i] = (wide_pot[i] + 6.0 * wide_pot[i + 1] + wide_pot[i + 2]) * 0.125
         rows_pot[2 * i + 1] = (wide_pot[i + 1] + wide_pot[i + 2]) * 0.5
-    below = rows_pot[:, 7:15]
-    middle = rows_pot[:, 8:16]
-    above = rows_pot[:, 9:17]
+    below = rows_pot[:, 0:8]
+    middle = rows_pot[:, 1:9]
+    above = rows_pot[:, 2:10]
     even_rows = (below + 6.0 * middle + above) * 0.125
     odd_rows = (middle + above) * 0.5
     for i in range(16):
@@ -517,19 +515,17 @@
         pltpu.VMEM((4, 4, 16, LZ), BF16),
         pltpu.VMEM((32, 32, LZ), F32),
         pltpu.VMEM((768, 2 * LZ), BF16),
-        pltpu.VMEM((8, 32, LZ), F32),
+        pltpu.VMEM((10, 32, LZ), F32),
         pltpu.VMEM((2, 4, 8, 24, LZ), F32),
         pltpu.VMEM((SIDE, 4, 16, STRIP), BF16),
         pltpu.VMEM((SIDE, 4, 16, STRIP), BF16),
-        pltpu.VMEM((2, 16, LZ), BF16),
-        pltpu.VMEM((8, 2, 16, LZ), BF16),
-        pltpu.VMEM((24, 32, LZ), F32),
+        pltpu.VMEM((10, 16, LZ), F32),
+        pltpu.VMEM((8, 3, 16, LZ), BF16),
+        pltpu.VMEM((8, 3, 16, LZ), BF16),
+        pltpu.VMEM((32, 32, LZ), F32),
         pltpu.VMEM((2, LZ, LZ), F32),
-        pltpu.VMEM((8, 8, LZ), F32),
-        pltpu.VMEM((2, 8, LZ), F32),
-        pltpu.VMEM((8, 8, LZ), F32),
-        pltpu.VMEM((10, 24, LZ), F32),
-        pltpu.VMEM((16, 24, LZ), F32),
+        pltpu.VMEM((10, 16, LZ), F32),
+        pltpu.VMEM((16, 16, LZ), F32),
         pltpu.VMEM((3, 16, LZ), F32),
         pltpu.VMEM((16, 16, LZ), F32),
         pltpu.VMEM((3, 16, LZ), F32),
@@ -537,7 +533,7 @@
         pltpu.VMEM((3, 8, LZ), F32),
         pltpu.VMEM((ROWS, 2 * LZ), BF16),
     ]
-    for count in (3, 8, 8, 8, 3):
+    for count in (3, 8, 8, 3):
         scratch += [dma((count,)), dma((count,))]
     bead, grid = pl.pallas_call(
         functools.partial(melt_kernel, sizes),

time: 52.6 us -> 48.5 us (0.922)
  Pallas kernels: 51.2 us -> 47.1 us
    pallas_call x1, Pallas kernels: 49.6 us -> 45.5 us  [on_device(): pl.pallas_call(functools.partial(melt_kernel, sizes), out_shape=(jax.Shap...]
where the time goes in v3:
time: 48.5 us; the launch traced here: 48.4 us
  Pallas kernels  47.1 us (97%)
  between operations  1.28 us (3%)
    pallas_call x1, Pallas kernels, on_device(): pl.pallas_call(functools.partial(melt_kernel, sizes), out_shape=(jax.Shap...  45.5 us
    pallas_call x1, Pallas kernels, on_device(): pl.pallas_call(hand_over, out_shape=(jax.ShapeDtypeStruct((1, slots), F32...  1.63 us

profile of v3, /device:TPU:1, one launch (start us, length us, event | category | flops | bytes accessed | tf_op | source)
XLA Modules:
  0.0 48.4 jit_solution(18096665131018938817)
XLA Ops:
  1.3 45.5 %melt.1 = (f32[1,16384]{1,0:T(1,128)}, f32[16,16,128]{2,1,0:T(8,128)}) custom-call(s32[1,1]{1,0:T(1,128)S(6)} %copy.8.count_ref, f32[1,16384]{1,0:T(1,128)} %bitcast.5, s32[1,16384]{1,0:T(1,128)} %bitcast.6, bf16[12,16384]{1,0:T(8,128)(2,1)} %bitcast.4, bf16[17,17,17]{2,1,0:T(8,128)(2,1)} %fine_hbm.1, bf16[17,17,17]{2,1,0:T(8,128)(2,1)} %coarse_hbm.1), custom_call_target="tpu_custom_call" | custom-call | tf_op jit(solution)/shard_map/melt/pallas_call | solution.py:538
  46.8 1.6 %hand_over.1 = (f32[1,16384]{1,0:T(1,128)}, f32[16,16,128]{2,1,0:T(8,128)}) custom-call(f32[1,16384]{1,0:T(1,128)} %get-tuple-element.6.bead_from, f32[16,16,128]{2,1,0:T(8,128)} %get-tuple-element.7.grid_from), custom_call_target="tpu_custom_call" | custom-call | tf_op jit(solution)/shard_map/hand_over/pallas_call | solution.py:552

commit v4 on v3

--- a/solution.py
+++ b/solution.py
@@ -12,6 +12,7 @@
 LZ = 128
 SIDE = 17
 BLOCK = 8192
+READ_BLOCK = 16384
 ROWS = 384
 STRIP = 1024
 GROUP = 5
@@ -20,7 +21,7 @@
 BF16 = jnp.bfloat16
 LANES_BOTH = (((1,), (1,)), ((), ()))
 ROWS_BOTH = (((0,), (0,)), ((), ()))
-AROUND = [(a, b) for a in (-1, 0, 1) for b in (-1, 0, 1) if (a, b) != (0, 0)]
+AROUND = [(a, b) for a in (-1, 1, 0) for b in (0, -1, 1) if (a, b) != (0, 0)]
 
 
 def iota(shape, dim):
@@ -80,6 +81,10 @@
     side_first,
     side_second,
     side_both,
+    beside,
+    beyond,
+    low_edge,
+    low_corner,
     charges,
     out_edge,
     out_corner,
@@ -159,9 +164,9 @@
     far_total[...] = jnp.zeros_like(far_total)
     near_total[...] = jnp.zeros_like(near_total)
 
-    def block_at(step):
-        start = pl.multiple_of(step * BLOCK, BLOCK)
-        return pl.ds(start, BLOCK), iota((1, BLOCK), 1) + start < live
+    def block_at(step, size):
+        start = pl.multiple_of(step * size, size)
+        return pl.ds(start, size), iota((1, size), 1) + start < live
 
     def add_rows(sums, parts, depth):
         high, low = split(jnp.concatenate(parts, axis=0))
@@ -171,7 +176,7 @@
         sums[...] += both[: high.shape[0]] + both[high.shape[0] :]
 
     def spread_far(step, carry):
-        here, alive = block_at(step)
+        here, alive = block_at(step, BLOCK)
         weights = weight_ref[:, here].astype(F32)
         rows_first, rows_second, depth = bead_tables(cell_ref[:, here], weights)
         all_first[:, here] = rows_first
@@ -185,7 +190,7 @@
         return carry
 
     def spread_near(step, carry):
-        here, alive = block_at(step)
+        here, alive = block_at(step, BLOCK)
         rows_first = all_first[0:16, here] * jnp.where(alive, charge_ref[:, here], 0.0)
         rows_second = all_second[0:16, here]
         parts = [rows_first[x : x + 1] * rows_second for x in range(16)]
@@ -199,38 +204,52 @@
 
     pl.semaphore_wait(barrier, 8)
 
-    spills = [
+    spills_first = [
         send(main_far, side_first, send_1.at[0], recv_1.at[0], 1, 0),
-        send(tail.at[:, 16:24], side_both, send_1.at[2], recv_1.at[2], 1, 1),
-        send(tail.at[:, 0:16], side_second, send_1.at[1], recv_1.at[1], 0, 1),
+        send(tail.at[:, 16:24], side_both, send_1.at[1], recv_1.at[1], 1, 1),
     ]
+    spills_second = [
+        send(tail, side_second, send_1.at[2], recv_1.at[2], 0, 1),
+        send(main_far.at[:, 8:16], beside.at[0], send_1.at[3], recv_1.at[3], 0, 1),
+        send(main_far.at[:, 0:8], beside.at[1], send_1.at[4], recv_1.at[4], 0, -1),
+    ]
 
     lax.fori_loop(0, steps, spread_near, 0)
 
-    for copy in spills:
+    for copy in spills_second:
         copy.wait()
     charges[...] = near_total[...].reshape(16, 16, LZ)
-    charges[0:3] += side_first[...]
+    beyond[:, 0:8] = beside[0]
+    beyond[:, 8:24] = main_far[...]
+    beyond[:, 24:32] = beside[1]
     for y in range(3):
-        side_second[y, 0:8] += side_both[y]
-        charges[:, y, :] += side_second[y]
+        charges[:, y, :] += side_second[y, 0:16]
+        beyond[:, 8 + y, :] += side_second[y, 16:19]
+        beyond[:, 24 + y, :] += tail[y, 16:19]
     grid[8:24, 8:24] = charges[...].astype(BF16).astype(F32)
 
-    out_edge[0] = grid[8:16, 8:24].astype(BF16)
+    out_edge[0, 3:8] = grid[11:16, 8:24].astype(BF16)
     out_edge[1] = grid[16:24, 8:24].astype(BF16)
-    out_edge[2] = grid[8:24, 8:16].reshape(8, 16, LZ).astype(BF16)
-    out_edge[3] = grid[8:24, 16:24].reshape(8, 16, LZ).astype(BF16)
     for i in range(2):
         for j in range(2):
             quarter = grid[8 + 8 * i : 16 + 8 * i, 8 + 8 * j : 16 + 8 * j]
             out_corner[2 * i + j] = quarter.reshape(4, 16, LZ).astype(BF16)
     halos = []
-    for at, (a, b) in enumerate([(-1, 0), (1, 0), (0, -1), (0, 1)]):
-        halos.append(send(out_edge.at[at], in_edge.at[at], send_2.at[at], recv_2.at[at], a, b))
-    for at, (a, b) in enumerate([(-1, -1), (-1, 1), (1, -1), (1, 1)]):
-        halos.append(
-            send(out_corner.at[at], in_corner.at[at], send_2.at[4 + at], recv_2.at[4 + at], a, b)
-        )
+    for at, (source, target, a, b) in enumerate(
+        [
+            (charges.at[0:3], low_edge, -1, 0),
+            (out_edge.at[1], in_edge.at[1], 1, 0),
+            (out_edge.at[0, 3:8], in_edge.at[0, 3:8], -1, 0),
+            (charges.at[0:3, 0:8], low_corner.at[0], -1, -1),
+            (charges.at[0:3, 8:16], low_corner.at[1], -1, 1),
+            (out_corner.at[2], in_corner.at[2], 1, -1),
+            (out_corner.at[3], in_corner.at[3], 1, 1),
+            (out_corner.at[0, 1:4], in_corner.at[0, 1:4], -1, -1),
+            (out_corner.at[1, 1:4], in_corner.at[1, 1:4], -1, 1),
+        ]
+    ):
+        halos.append(send(source, target, send_2.at[at], recv_2.at[at], a, b))
+
     lanes = iota((SIDE, LZ), 1)
     taps = iota((SIDE, LZ), 0)
     for at, source in enumerate((fine_ref, coarse_ref)):
@@ -273,16 +292,31 @@
     lax.fori_loop(0, SIDE, build, 0)
     wide_coarse[...] = jnp.zeros_like(wide_coarse)
 
+    for copy in spills_first:
+        copy.wait()
+    for y in range(3):
+        side_first[:, y, :] += side_both[y, 0:3]
+    grid[8:11, 8:24] = (charges[0:3] + side_first[...]).astype(BF16).astype(F32)
+    out_edge[2] = grid[8:24, 8:16].reshape(8, 16, LZ).astype(BF16)
+    out_edge[3] = grid[8:24, 16:24].reshape(8, 16, LZ).astype(BF16)
+    for at, b in ((2, -1), (3, 1)):
+        halos.append(
+            send(out_edge.at[at], in_edge.at[at], send_2.at[7 + at], recv_2.at[7 + at], 0, b)
+        )
     for copy in halos:
         copy.wait()
-    grid[24:32, 8:24] = in_edge[0].astype(F32)
+    grid[27:32, 8:24] = in_edge[0, 3:8].astype(F32)
+    grid[24:27, 8:24] = (low_edge[...] + beyond[:, 8:24]).astype(BF16).astype(F32)
+    grid[24:27, 24:32] = (low_corner[0] + beyond[:, 24:32]).astype(BF16).astype(F32)
+    grid[24:27, 0:8] = (low_corner[1] + beyond[:, 0:8]).astype(BF16).astype(F32)
     grid[0:8, 8:24] = in_edge[1].astype(F32)
     grid[8:24, 24:32] = in_edge[2].astype(F32).reshape(16, 8, LZ)
     grid[8:24, 0:8] = in_edge[3].astype(F32).reshape(16, 8, LZ)
-    for i in range(2):
-        for j in range(2):
-            quarter = in_corner[2 * i + j].astype(F32).reshape(8, 8, LZ)
-            grid[24 - 24 * i : 32 - 24 * i, 24 - 24 * j : 32 - 24 * j] = quarter
+    for j in range(2):
+        y = 24 - 24 * j
+        upper_quarter = in_corner[j, 1:4].astype(F32).reshape(6, 8, LZ)
+        grid[27:32, y : y + 8] = upper_quarter[1:6]
+        grid[0:8, y : y + 8] = in_corner[2 + j].astype(F32).reshape(8, 8, LZ)
 
     gap = (iota((LZ, LZ), 0) - 2 * (iota((LZ, LZ), 1) & 63) + 2) & 127
     spline = jnp.where(gap == 2, 0.75, 0.0)
@@ -426,21 +460,23 @@
 
     put_table(0, potential[...].reshape(256, LZ))
 
+    slots = charge_ref.shape[1]
+
     def read_near(step, carry):
-        here, _ = block_at(step)
+        here, _ = block_at(step, READ_BLOCK)
         depth = all_depth[:, here]
         along = jnp.dot(
             read_table[0:256], jnp.concatenate([depth, depth], axis=0), preferred_element_type=F32
         )
         rows_first = all_first[:, here]
-        near = jnp.zeros((16, BLOCK), F32)
+        near = jnp.zeros((16, READ_BLOCK), F32)
         for x in range(16):
             near = near + rows_first[x : x + 1] * along[16 * x : 16 * x + 16]
         near = near * all_second[0:16, here]
         bead_ref[:, here] = jnp.sum(near[:8] + near[8:], axis=0, keepdims=True)
         return carry
 
-    lax.fori_loop(0, steps, read_near, 0)
+    lax.fori_loop(0, slots // READ_BLOCK, read_near, 0)
 
     for copy in upper:
         copy.wait()
@@ -452,7 +488,7 @@
     put_table(304, jnp.concatenate(ends, axis=0))
 
     def read_far(step, carry):
-        here, alive = block_at(step)
+        here, alive = block_at(step, READ_BLOCK)
         depth = all_depth[:, here]
         along = jnp.dot(
             read_table[256:384],
@@ -461,10 +497,10 @@
         )
         rows_first = all_first[:, here]
         rows_second = all_second[:, here]
-        near = jnp.zeros((16, BLOCK), F32)
+        near = jnp.zeros((16, READ_BLOCK), F32)
         for x in range(3):
             near = near + rows_first[16 + x : 17 + x] * along[16 * x : 16 * x + 16]
-        far = jnp.zeros((24, BLOCK), F32)
+        far = jnp.zeros((24, READ_BLOCK), F32)
         for y in range(3):
             far = far + rows_second[16 + y : 17 + y] * along[48 + 24 * y : 72 + 24 * y]
         near = near * rows_second[:16]
@@ -474,7 +510,7 @@
         bead_ref[:, here] = jnp.where(alive, value, 0.0)
         return carry
 
-    lax.fori_loop(0, steps, read_far, 0)
+    lax.fori_loop(0, slots // READ_BLOCK, read_far, 0)
 
 
 def hand_over(bead_from, grid_from, bead_to, grid_to):
@@ -506,8 +542,12 @@
         pltpu.VMEM((3, 16, LZ), F32),
         pltpu.VMEM((3, 24, LZ), F32),
         pltpu.VMEM((3, 16, LZ), F32),
+        pltpu.VMEM((3, 24, LZ), F32),
+        pltpu.VMEM((3, 8, LZ), F32),
+        pltpu.VMEM((2, 3, 8, LZ), F32),
+        pltpu.VMEM((3, 32, LZ), F32),
         pltpu.VMEM((3, 16, LZ), F32),
-        pltpu.VMEM((3, 8, LZ), F32),
+        pltpu.VMEM((2, 3, 8, LZ), F32),
         pltpu.VMEM((16, 16, LZ), F32),
         pltpu.VMEM((4, 8, 16, LZ), BF16),
         pltpu.VMEM((4, 4, 16, LZ), BF16),
@@ -533,7 +573,7 @@
         pltpu.VMEM((3, 8, LZ), F32),
         pltpu.VMEM((ROWS, 2 * LZ), BF16),
     ]
-    for count in (3, 8, 8, 3):
+    for count in (5, 11, 8, 3):
         scratch += [dma((count,)), dma((count,))]
     bead, grid = pl.pallas_call(
         functools.partial(melt_kernel, sizes),

time: 48.5 us -> 45 us (0.928)
  Pallas kernels: 47.1 us -> 43.6 us
    pallas_call x1, Pallas kernels: 45.5 us -> 41.9 us  [on_device(): pl.pallas_call(functools.partial(melt_kernel, sizes), out_shape=(jax.Shap...]
where the time goes in v4:
time: 45 us; the launch traced here: 44.9 us
  Pallas kernels  43.6 us (97%)
  between operations  1.28 us (3%)
    pallas_call x1, Pallas kernels, on_device(): pl.pallas_call(functools.partial(melt_kernel, sizes), out_shape=(jax.Shap...  41.9 us
    pallas_call x1, Pallas kernels, on_device(): pl.pallas_call(hand_over, out_shape=(jax.ShapeDtypeStruct((1, slots), F32...  1.63 us

profile of v4, /device:TPU:1, one launch (start us, length us, event | category | flops | bytes accessed | tf_op | source)
XLA Modules:
  0.0 44.9 jit_solution(12157677901201409822)
XLA Ops:
  1.3 41.9 %melt.1 = (f32[1,16384]{1,0:T(1,128)}, f32[16,16,128]{2,1,0:T(8,128)}) custom-call(s32[1,1]{1,0:T(1,128)S(6)} %copy.8.count_ref, f32[1,16384]{1,0:T(1,128)} %bitcast.5, s32[1,16384]{1,0:T(1,128)} %bitcast.6, bf16[12,16384]{1,0:T(8,128)(2,1)} %bitcast.4, bf16[17,17,17]{2,1,0:T(8,128)(2,1)} %fine_hbm.1, bf16[17,17,17]{2,1,0:T(8,128)(2,1)} %coarse_hbm.1), custom_call_target="tpu_custom_call" | custom-call | tf_op jit(solution)/shard_map/melt/pallas_call | solution.py:578
  43.2 1.6 %hand_over.1 = (f32[1,16384]{1,0:T(1,128)}, f32[16,16,128]{2,1,0:T(8,128)}) custom-call(f32[1,16384]{1,0:T(1,128)} %get-tuple-element.6.bead_from, f32[16,16,128]{2,1,0:T(8,128)} %get-tuple-element.7.grid_from), custom_call_target="tpu_custom_call" | custom-call | tf_op jit(solution)/shard_map/hand_over/pallas_call | solution.py:592

commit v5 on v4

--- a/solution.py
+++ b/solution.py
@@ -11,11 +11,12 @@
 LY = 16
 LZ = 128
 SIDE = 17
-BLOCK = 8192
+FAR_BLOCK = 16384
+NEAR_BLOCK = 16384
 READ_BLOCK = 16384
 ROWS = 384
 STRIP = 1024
-GROUP = 5
+GROUP = 9
 MESH = pl.DeviceIdType.MESH
 F32 = jnp.float32
 BF16 = jnp.bfloat16
@@ -176,7 +177,7 @@
         sums[...] += both[: high.shape[0]] + both[high.shape[0] :]
 
     def spread_far(step, carry):
-        here, alive = block_at(step, BLOCK)
+        here, alive = block_at(step, FAR_BLOCK)
         weights = weight_ref[:, here].astype(F32)
         rows_first, rows_second, depth = bead_tables(cell_ref[:, here], weights)
         all_first[:, here] = rows_first
@@ -185,20 +186,20 @@
         rows_first = rows_first * jnp.where(alive, charge_ref[:, here], 0.0)
         parts = [rows_first[x : x + 1] * rows_second[:16] for x in range(16, 19)]
         parts += [rows_second[y : y + 1] * rows_first for y in range(16, 19)]
-        parts += [jnp.zeros((8, BLOCK), F32)]
+        parts += [jnp.zeros((8, FAR_BLOCK), F32)]
         add_rows(far_total, parts, depth)
         return carry
 
     def spread_near(step, carry):
-        here, alive = block_at(step, BLOCK)
+        here, alive = block_at(step, NEAR_BLOCK)
         rows_first = all_first[0:16, here] * jnp.where(alive, charge_ref[:, here], 0.0)
         rows_second = all_second[0:16, here]
         parts = [rows_first[x : x + 1] * rows_second for x in range(16)]
         add_rows(near_total, parts, all_depth[:, here])
         return carry
 
-    steps = charge_ref.shape[1] // BLOCK
-    lax.fori_loop(0, steps, spread_far, 0)
+    slots = charge_ref.shape[1]
+    lax.fori_loop(0, slots // FAR_BLOCK, spread_far, 0)
     main_far[...] = far_total[0:48].reshape(3, 16, LZ)
     tail[...] = far_total[48:120].reshape(3, 24, LZ)
 
@@ -214,7 +215,7 @@
         send(main_far.at[:, 0:8], beside.at[1], send_1.at[4], recv_1.at[4], 0, -1),
     ]
 
-    lax.fori_loop(0, steps, spread_near, 0)
+    lax.fori_loop(0, slots // NEAR_BLOCK, spread_near, 0)
 
     for copy in spills_second:
         copy.wait()
@@ -386,9 +387,10 @@
 
     correlate_fine(0, SIDE)
 
-    for copy in coarse_sends:
+    for at in (6, 7, 0, 1, 2, 3, 4, 5):
+        copy = coarse_sends[at]
         copy.wait()
-    for at, (a, b) in enumerate(AROUND):
+        a, b = AROUND[at]
         x, y = 9 - 8 * a, 9 - 8 * b
         for k in range(2):
             pair_rows = in_coarse[at, k].astype(F32)
@@ -459,8 +461,6 @@
         read_table[start : start + rows.shape[0], LZ:] = low
 
     put_table(0, potential[...].reshape(256, LZ))
-
-    slots = charge_ref.shape[1]
 
     def read_near(step, carry):
         here, _ = block_at(step, READ_BLOCK)

time: 45 us -> 50 us (1.11)
  Pallas kernels: 43.6 us -> 48.6 us
    pallas_call x1, Pallas kernels: 41.9 us -> 46.9 us  [on_device(): pl.pallas_call(functools.partial(melt_kernel, sizes), out_shape=(jax.Shap...]
where the time goes in v5:
time: 50 us; the launch traced here: 49.9 us
  Pallas kernels  48.6 us (97%)
  between operations  1.28 us (3%)
    pallas_call x1, Pallas kernels, on_device(): pl.pallas_call(functools.partial(melt_kernel, sizes), out_shape=(jax.Shap...  46.9 us
    pallas_call x1, Pallas kernels, on_device(): pl.pallas_call(hand_over, out_shape=(jax.ShapeDtypeStruct((1, slots), F32...  1.63 us

profile of v5, /device:TPU:1, one launch (start us, length us, event | category | flops | bytes accessed | tf_op | source)
XLA Modules:
  0.0 49.9 jit_solution(14279789863906376517)
XLA Ops:
  1.3 46.9 %melt.1 = (f32[1,16384]{1,0:T(1,128)}, f32[16,16,128]{2,1,0:T(8,128)}) custom-call(s32[1,1]{1,0:T(1,128)S(6)} %copy.8.count_ref, f32[1,16384]{1,0:T(1,128)} %bitcast.5, s32[1,16384]{1,0:T(1,128)} %bitcast.6, bf16[12,16384]{1,0:T(8,128)(2,1)} %bitcast.4, bf16[17,17,17]{2,1,0:T(8,128)(2,1)} %fine_hbm.1, bf16[17,17,17]{2,1,0:T(8,128)(2,1)} %coarse_hbm.1), custom_call_target="tpu_custom_call" | custom-call | tf_op jit(solution)/shard_map/melt/pallas_call | solution.py:578
  48.2 1.6 %hand_over.1 = (f32[1,16384]{1,0:T(1,128)}, f32[16,16,128]{2,1,0:T(8,128)}) custom-call(f32[1,16384]{1,0:T(1,128)} %get-tuple-element.6.bead_from, f32[16,16,128]{2,1,0:T(8,128)} %get-tuple-element.7.grid_from), custom_call_target="tpu_custom_call" | custom-call | tf_op jit(solution)/shard_map/hand_over/pallas_call | solution.py:592

commit v6 on v5

--- a/solution.py
+++ b/solution.py
@@ -11,12 +11,12 @@
 LY = 16
 LZ = 128
 SIDE = 17
-FAR_BLOCK = 16384
-NEAR_BLOCK = 16384
+FAR_BLOCK = 8192
+NEAR_BLOCK = 8192
 READ_BLOCK = 16384
 ROWS = 384
 STRIP = 1024
-GROUP = 9
+GROUP = 5
 MESH = pl.DeviceIdType.MESH
 F32 = jnp.float32
 BF16 = jnp.bfloat16

time: 50 us -> 45 us (0.900)
  Pallas kernels: 48.6 us -> 43.6 us
    pallas_call x1, Pallas kernels: 46.9 us -> 42 us  [on_device(): pl.pallas_call(functools.partial(melt_kernel, sizes), out_shape=(jax.Shap...]
where the time goes in v6:
time: 45 us; the launch traced here: 44.9 us
  Pallas kernels  43.6 us (97%)
  between operations  1.28 us (3%)
    pallas_call x1, Pallas kernels, on_device(): pl.pallas_call(functools.partial(melt_kernel, sizes), out_shape=(jax.Shap...  42 us
    pallas_call x1, Pallas kernels, on_device(): pl.pallas_call(hand_over, out_shape=(jax.ShapeDtypeStruct((1, slots), F32...  1.63 us

profile of v6, /device:TPU:1, one launch (start us, length us, event | category | flops | bytes accessed | tf_op | source)
XLA Modules:
  0.0 44.9 jit_solution(17777347536333134654)
XLA Ops:
  1.3 42.0 %melt.1 = (f32[1,16384]{1,0:T(1,128)}, f32[16,16,128]{2,1,0:T(8,128)}) custom-call(s32[1,1]{1,0:T(1,128)S(6)} %copy.8.count_ref, f32[1,16384]{1,0:T(1,128)} %bitcast.5, s32[1,16384]{1,0:T(1,128)} %bitcast.6, bf16[12,16384]{1,0:T(8,128)(2,1)} %bitcast.4, bf16[17,17,17]{2,1,0:T(8,128)(2,1)} %fine_hbm.1, bf16[17,17,17]{2,1,0:T(8,128)(2,1)} %coarse_hbm.1), custom_call_target="tpu_custom_call" | custom-call | tf_op jit(solution)/shard_map/melt/pallas_call | solution.py:578
  43.3 1.6 %hand_over.1 = (f32[1,16384]{1,0:T(1,128)}, f32[16,16,128]{2,1,0:T(8,128)}) custom-call(f32[1,16384]{1,0:T(1,128)} %get-tuple-element.6.bead_from, f32[16,16,128]{2,1,0:T(8,128)} %get-tuple-element.7.grid_from), custom_call_target="tpu_custom_call" | custom-call | tf_op jit(solution)/shard_map/hand_over/pallas_call | solution.py:592
